TPU v7x, 256 devices: a whole 4x4x8 slice. The times are simulated.
256 devices in a mesh: ctx: 64 (over y, z_hi, x, core), rep: 4 (over z_lo).
Axes of the slice: x: 4, y: 4, z: 8 (z_hi: 2, z_lo: 4; z = z_hi * 4 + z_lo), core: 2. Of those that a mesh axis runs over, the one named last changes fastest.
Arguments:
- features: bfloat16 [3, 16, 512, 8192], P(None, 'rep', None, 'ctx'), may hold values from -6 to 6
- short_taps: float32 [3, 16, 512, 3], P(None, 'rep'), may hold values from -3.5 to 3.5
- skip_gain: float32 [16, 512], P('rep', 'ctx'), may hold values from -4 to 4
- filters: float32 [512, 8192], P('ctx'), may hold values from -4 to 4
- cotangent: bfloat16 [16, 512, 8192], P('rep', None, 'ctx'), may hold values from -16 to 16
Outputs:
- d_features: bfloat16 [3, 16, 512, 8192], P(None, 'rep', None, 'ctx')
- d_short: float32 [3, 16, 512, 3], P(None, 'rep', 'ctx')
- d_skip: float32 [16, 512], P('rep', 'ctx')
- d_filter: float32 [512, 8192], P('ctx', 'rep')
All inputs are finite; a program needn't handle non-finite values.
Results may differ from a plain program's by a relative error of at most 0.014.
Values may be sent and summed in bfloat16 or wider, within the bound.
A program may use at most 256 MiB of HBM per device.

v0:
```python
import math

import jax
import jax.numpy as jnp
from jax import lax
from jax.sharding import PartitionSpec as P

dft_mode = lax.Precision.HIGH


def shifted(block, axis, distance):
    devices = range(lax.axis_size(axis))
    route = [(i - distance, i) for i in devices if i - distance in devices]
    return lax.ppermute(block, axis, route)


def square_table(count):
    index = jnp.arange(count, dtype=jnp.int32)
    angle = (index[:, None] * index[None, :] % count).astype(jnp.float32) * (2.0 * math.pi / count)
    return (jnp.cos(angle), jnp.sin(angle))


def make_plan(length):
    total = 2 * length
    outer = min(128, total)
    inner = total // outer
    outer_cos, outer_sin = square_table(outer)
    inner_cos, inner_sin = square_table(inner)
    rows_index = jnp.arange(outer, dtype=jnp.int32)[:, None]
    cols_index = jnp.arange(inner, dtype=jnp.int32)[None, :]
    angle = (rows_index * cols_index % total).astype(jnp.float32) * (2.0 * math.pi / total)
    return (
        outer_cos,
        outer_sin,
        jnp.cos(angle),
        jnp.sin(angle),
        inner_cos,
        inner_sin,
        outer,
        inner,
    )


def spectrum(signal, plan):
    outer_cos, outer_sin, twist_cos, twist_sin, inner_cos, inner_sin, outer, inner = plan
    half = outer // 2
    grid = signal.reshape(-1, half, inner)
    first_re = jnp.einsum("kn,bnq->bkq", outer_cos[:, :half], grid, precision=dft_mode)
    first_im = -jnp.einsum("kn,bnq->bkq", outer_sin[:, :half], grid, precision=dft_mode)
    turned_re = (first_re * twist_cos + first_im * twist_sin).reshape(-1, inner)
    turned_im = (first_im * twist_cos - first_re * twist_sin).reshape(-1, inner)
    out_re = jnp.dot(turned_re, inner_cos, precision=dft_mode) + jnp.dot(
        turned_im, inner_sin, precision=dft_mode
    )
    out_im = jnp.dot(turned_im, inner_cos, precision=dft_mode) - jnp.dot(
        turned_re, inner_sin, precision=dft_mode
    )
    return (out_re.reshape(-1, outer, inner), out_im.reshape(-1, outer, inner))


def signal_back(spec_re, spec_im, plan):
    outer_cos, outer_sin, twist_cos, twist_sin, inner_cos, inner_sin, outer, inner = plan
    half = outer // 2
    flat_re = spec_re.reshape(-1, inner)
    flat_im = spec_im.reshape(-1, inner)
    mid_re = (
        jnp.dot(flat_re, inner_cos, precision=dft_mode)
        - jnp.dot(flat_im, inner_sin, precision=dft_mode)
    ).reshape(-1, outer, inner)
    mid_im = (
        jnp.dot(flat_im, inner_cos, precision=dft_mode)
        + jnp.dot(flat_re, inner_sin, precision=dft_mode)
    ).reshape(-1, outer, inner)
    turned_re = mid_re * twist_cos - mid_im * twist_sin
    turned_im = mid_im * twist_cos + mid_re * twist_sin
    grid = jnp.einsum("nk,bkq->bnq", outer_cos[:half], turned_re, precision=dft_mode) - jnp.einsum(
        "nk,bkq->bnq", outer_sin[:half], turned_im, precision=dft_mode
    )
    return grid.reshape(-1, half * inner) / (outer * inner)


def short_forward(signal, taps):
    zeros = jnp.zeros(signal.shape[:-1] + (2,), jnp.float32)
    padded = jnp.concatenate([zeros, signal], axis=-1)
    length = signal.shape[-1]
    return (
        taps[..., 0:1] * signal
        + taps[..., 1:2] * padded[..., 1 : 1 + length]
        + taps[..., 2:3] * padded[..., 0:length]
    )


def short_backward(grads, taps):
    zeros = jnp.zeros(grads.shape[:-1] + (2,), jnp.float32)
    padded = jnp.concatenate([grads, zeros], axis=-1)
    length = grads.shape[-1]
    return (
        taps[..., 0:1] * grads
        + taps[..., 1:2] * padded[..., 1 : 1 + length]
        + taps[..., 2:3] * padded[..., 2 : 2 + length]
    )


def short_taps_grad(grads, signal):
    zeros = jnp.zeros(signal.shape[:-1] + (2,), jnp.float32)
    padded = jnp.concatenate([zeros, signal], axis=-1)
    length = signal.shape[-1]
    return jnp.stack(
        [
            jnp.sum(grads * signal, axis=-1),
            jnp.sum(grads * padded[..., 1 : 1 + length], axis=-1),
            jnp.sum(grads * padded[..., 0:length], axis=-1),
        ],
        axis=-1,
    )


def channel_work(product, gated_part, filters, skip_gain, plan):
    groups_here, filt_here, length = product.shape
    outer, inner = (plan[6], plan[7])
    value_sig = product.astype(jnp.float32)
    grad_sig = gated_part.astype(jnp.float32)
    filt_re, filt_im = spectrum(filters, plan)
    val_re, val_im = spectrum(value_sig.reshape(-1, length), plan)
    grd_re, grd_im = spectrum(grad_sig.reshape(-1, length), plan)
    shape_four = (groups_here, filt_here, outer, inner)
    val_re = val_re.reshape(shape_four)
    val_im = val_im.reshape(shape_four)
    grd_re = grd_re.reshape(shape_four)
    grd_im = grd_im.reshape(shape_four)
    conv_re = filt_re * val_re - filt_im * val_im
    conv_im = filt_re * val_im + filt_im * val_re
    corr_re = filt_re * grd_re + filt_im * grd_im
    corr_im = filt_re * grd_im - filt_im * grd_re
    skip_col = skip_gain[..., None]
    conv_back = signal_back(conv_re, conv_im, plan).reshape(groups_here, filt_here, length)
    corr_back = signal_back(corr_re, corr_im, plan).reshape(groups_here, filt_here, length)
    conv_full = lax.optimization_barrier((conv_back + skip_col * value_sig).astype(jnp.bfloat16))
    value_grad = lax.optimization_barrier((corr_back + skip_col * grad_sig).astype(jnp.bfloat16))
    lag_re = jnp.sum(grd_re * val_re + grd_im * val_im, axis=0)
    lag_im = jnp.sum(grd_im * val_re - grd_re * val_im, axis=0)
    skip_grad = jnp.sum(grad_sig * value_sig, axis=-1)
    return (conv_full, value_grad, lag_re, lag_im, skip_grad)


def per_device(features, short_taps, skip_gain, filters, cotangent):
    shards = lax.axis_size("ctx")
    tok_here = features.shape[3]
    filt_here = features.shape[2] // shards
    length = tok_here * shards
    plan = make_plan(length)
    cot_full = cotangent.astype(jnp.float32)
    taps_local = lax.dynamic_slice_in_dim(
        short_taps, lax.axis_index("ctx") * filt_here, filt_here, 2
    )
    front = features[0:1]
    front_taps = short_taps[0:1]
    before = shifted(front[..., tok_here - 2 :], "ctx", 1)
    front_ext = jnp.concatenate([before, front], axis=-1).astype(jnp.float32)
    front_mixed = (
        front_taps[..., 0:1] * front_ext[..., 2:]
        + front_taps[..., 1:2] * front_ext[..., 1 : tok_here + 1]
        + front_taps[..., 2:3] * front_ext[..., 0:tok_here]
    )
    gated = lax.optimization_barrier((cot_full * front_mixed[0]).astype(jnp.bfloat16))
    key_part, value_part, gated_part = (
        lax.all_to_all(features[1], "ctx", split_axis=1, concat_axis=2, tiled=True),
        lax.all_to_all(features[2], "ctx", split_axis=1, concat_axis=2, tiled=True),
        lax.all_to_all(gated, "ctx", split_axis=1, concat_axis=2, tiled=True),
    )
    key_sig = key_part.astype(jnp.float32)
    value_sig = value_part.astype(jnp.float32)
    key_mixed = short_forward(key_sig, taps_local[1])
    value_mixed = short_forward(value_sig, taps_local[2])
    product = lax.optimization_barrier((key_mixed * value_mixed).astype(jnp.bfloat16))
    conv_full, value_grad, lag_re, lag_im, skip_grad = channel_work(
        product, gated_part, filters, skip_gain, plan
    )
    grad_wide = value_grad.astype(jnp.float32)
    key_grad = grad_wide * value_mixed
    value_grad_ch = grad_wide * key_mixed
    taps_kv = jnp.stack(
        [short_taps_grad(key_grad, key_sig), short_taps_grad(value_grad_ch, value_sig)]
    )
    key_back = short_backward(key_grad, taps_local[1]).astype(jnp.bfloat16)
    value_back = short_backward(value_grad_ch, taps_local[2]).astype(jnp.bfloat16)
    conv_seq, key_seq, value_seq = (
        lax.all_to_all(conv_full, "ctx", split_axis=2, concat_axis=1, tiled=True),
        lax.all_to_all(key_back, "ctx", split_axis=2, concat_axis=1, tiled=True),
        lax.all_to_all(value_back, "ctx", split_axis=2, concat_axis=1, tiled=True),
    )
    grads = (cot_full * conv_seq.astype(jnp.float32))[None]
    after = shifted(grads[..., 0:2], "ctx", -1)
    grad_ext = jnp.concatenate([grads, after], axis=-1)
    front_back = (
        front_taps[..., 0:1] * grads
        + front_taps[..., 1:2] * grad_ext[..., 1 : tok_here + 1]
        + front_taps[..., 2:3] * grad_ext[..., 2 : tok_here + 2]
    )
    tap_terms = jnp.stack(
        [
            jnp.sum(grads * front_ext[..., 2:], axis=-1),
            jnp.sum(grads * front_ext[..., 1 : tok_here + 1], axis=-1),
            jnp.sum(grads * front_ext[..., 0:tok_here], axis=-1),
        ],
        axis=-1,
    )
    tap_share = lax.psum_scatter(tap_terms, "ctx", scatter_dimension=2, tiled=True)
    d_short = jnp.concatenate([tap_share, taps_kv], axis=0)
    d_features = jnp.stack([front_back[0].astype(jnp.bfloat16), key_seq, value_seq])
    lag_terms = signal_back(lag_re, lag_im, plan)
    d_filter = lax.psum_scatter(
        lag_terms.astype(jnp.bfloat16), "rep", scatter_dimension=1, tiled=True
    ).astype(jnp.float32)
    return (d_features, d_short, skip_grad, d_filter)


def solution(mesh):
    placed = (
        P(None, "rep", None, "ctx"),
        P(None, "rep", None, None),
        P("rep", "ctx"),
        P("ctx", None),
        P("rep", None, "ctx"),
    )
    return jax.shard_map(
        per_device,
        mesh=mesh,
        in_specs=placed,
        out_specs=(
            P(None, "rep", None, "ctx"),
            P(None, "rep", "ctx", None),
            P("rep", "ctx"),
            P("ctx", "rep"),
        ),
        check_vma=False,
    )
```

profile of v0, /device:TPU:32, one launch (start us, length us, event | category | flops | bytes accessed | tf_op | source)
XLA Modules:
  0.0 761.5 jit_solution(3383429019652745120)
XLA Ops:
  7.2 1.3 slice.170
  8.5 2.5 collective-permute-start.1
  11.0 2.3 fusion.232
  14.5 14.0 %all-to-all-start.1 = ((bf16[4,512,128]{2,0,1:T(4,128)(2,1)}), bf16[4,512,128]{2,0,1:T(4,128)(2,1)S(1)}, u32[]{:S(2)}, u32[]{:S(2)}) async-start(bf16[4,512,128]{2,0,1:T(4,128)(2,1)} %bitcast.261), calls=%async_computation.1 | async-start | bytes 1048576 | tf_op jit(solution)/shard_map/all_to_all | solution.py:168
  29.7 1.2 copy.198
  33.2 17.2 %all-to-all-done.1 = bf16[4,512,128]{2,0,1:T(4,128)(2,1)S(1)} async-done(((bf16[4,512,128]{2,0,1:T(4,128)(2,1)}), bf16[4,512,128]{2,0,1:T(4,128)(2,1)S(1)}, u32[]{:S(2)}, u32[]{:S(2)}) %all-to-all-start.1) | async-done | bytes 524320 | tf_op jit(solution)/shard_map/all_to_all | solution.py:168
  50.4 5.5 all-to-all-start
  56.0 1.4 convolution_subtract_fusion.5
  58.7 1.6 maximum_convert_fusion
  60.4 2.5 fusion.45
  64.1 11.8 %all-to-all-done = bf16[4,512,128]{2,0,1:T(4,128)(2,1)} async-done(((bf16[4,512,128]{2,0,1:T(4,128)(2,1)}), bf16[4,512,128]{2,0,1:T(4,128)(2,1)}, u32[]{:S(2)}, u32[]{:S(2)}) %all-to-all-start) | async-done | bytes 524320 | tf_op jit(solution)/shard_map/all_to_all | solution.py:167
  75.9 5.5 all-to-all-start.3
  82.5 1.4 convolution_add_fusion.5
  88.4 12.4 %all-to-all-done.3 = bf16[4,512,128]{2,0,1:T(4,128)(2,1)} async-done(((bf16[4,512,128]{2,0,1:T(4,128)(2,1)}), bf16[4,512,128]{2,0,1:T(4,128)(2,1)}, u32[]{:S(2)}, u32[]{:S(2)}) %all-to-all-start.3) | async-done | bytes 524320 | tf_op jit(solution)/shard_map/all_to_all | solution.py:169
  100.8 1.2 copy.154
  107.8 2.8 fusion.3
  110.6 1.2 fusion.99
  111.9 1.2 fusion.101
  113.1 1.4 convolution_add_fusion
  114.6 1.2 convolution_subtract_fusion
  116.8 2.0 fusion.33
  118.7 2.4 div.25
  121.1 1.7 fusion.49
  123.1 7.2 multiply_reduce_fusion.4
  132.5 1.2 fusion.115
  133.8 1.2 fusion.111
  135.1 1.2 convolution_add_fusion.3
  137.5 5.3 multiply_add_fusion
  142.8 1.8 reduce_sum.118
  144.6 1.4 fusion.97
  146.0 1.8 reduce_sum.119
  148.4 1.7 convolution_subtract_fusion.4
  150.1 1.7 convolution_add_fusion.4
  153.2 3.4 fusion.107
  156.6 1.2 fusion.109
  157.8 1.2 convolution_add_fusion.2
  161.6 1.9 fusion.39
  163.5 2.5 div.22
  166.0 2.3 fusion.50
  168.3 8.1 %copy.126 = bf16[4,8,8192]{1,0,2:T(4,128)(2,1)} copy(bf16[4,8,8192]{2,1,0:T(8,128)(2,1)S(1)} %get-tuple-element.45) | data formatting | bytes 1048576 | tf_op jit(solution)/shard_map/optimization_barrier | solution.py:138
  176.4 11.3 %reshape.219 = bf16[64,2,2048]{2,1,0:T(2,128)(2,1)} reshape(bf16[8192,4,8]{2,1,0:T(4,128)(2,1)} %bitcast.267) | data formatting | bytes 1048576
  187.7 5.5 all-to-all-start.2
  193.2 1.4 add_convert_fusion.1
  194.6 9.6 %copy.136 = bf16[4,8,8192]{1,0,2:T(4,128)(2,1)} copy(bf16[4,8,8192]{2,1,0:T(8,128)(2,1)} %add_convert_fusion.1) | data formatting | bytes 1048576 | tf_op jit(solution)/shard_map/convert_element_type | solution.py:185
  204.3 11.3 %reshape.217 = bf16[64,2,2048]{2,1,0:T(2,128)(2,1)} reshape(bf16[8192,4,8]{2,1,0:T(4,128)(2,1)} %bitcast.268) | data formatting | bytes 1048576
  215.6 13.1 %all-to-all-start.4 = ((bf16[64,2,2048]{2,1,0:T(2,128)(2,1)}), bf16[64,2,2048]{2,1,0:T(2,128)(2,1)}, u32[]{:S(2)}, u32[]{:S(2)}) async-start(bf16[64,2,2048]{2,1,0:T(2,128)(2,1)} %reshape.217), calls=%async_computation.4 | async-start | bytes 1048576 | tf_op jit(solution)/shard_map/all_to_all | solution.py:189
  228.7 1.4 add_convert_fusion
  230.1 9.6 %copy.139 = bf16[4,8,8192]{1,0,2:T(4,128)(2,1)} copy(bf16[4,8,8192]{2,1,0:T(8,128)(2,1)} %add_convert_fusion) | data formatting | bytes 1048576 | tf_op jit(solution)/shard_map/convert_element_type | solution.py:186
  239.7 11.2 %reshape.215 = bf16[64,2,2048]{2,1,0:T(2,128)(2,1)} reshape(bf16[8192,4,8]{2,1,0:T(4,128)(2,1)} %bitcast.269) | data formatting | bytes 1048576
  251.0 13.1 %all-to-all-start.5 = ((bf16[64,2,2048]{2,1,0:T(2,128)(2,1)}), bf16[64,2,2048]{2,1,0:T(2,128)(2,1)}, u32[]{:S(2)}, u32[]{:S(2)}) async-start(bf16[64,2,2048]{2,1,0:T(2,128)(2,1)} %reshape.215), calls=%async_computation.5 | async-start | bytes 1048576 | tf_op jit(solution)/shard_map/all_to_all | solution.py:190
  264.2 1.4 convert_element_type.256
  265.6 11.6 %reshape.220 = bf16[8192,4,8]{2,1,0:T(4,128)(2,1)} reshape(bf16[64,2,2048]{2,1,0:T(2,128)(2,1)} %all-to-all-done.2) | data formatting | bytes 1048576
  277.2 9.7 %copy.127 = bf16[4,8,8192]{2,1,0:T(8,128)(2,1)S(1)} copy(bf16[4,8,8192]{1,0,2:T(4,128)(2,1)} %bitcast.270) | data formatting | bytes 1048576 | tf_op jit(solution)/shard_map/all_to_all | solution.py:188
  288.0 2.4 multiply_reduce_fusion.8
  290.4 1.6 copy.129
  291.9 1.3 collective-permute-start
  293.2 410.6 %all-reduce.4 = f32[1,4,512,3]{2,1,3,0:T(4,128)S(1)} all-reduce(f32[1,4,512,3]{2,1,3,0:T(4,128)S(1)} %pad_maximum_fusion.2), channel_id=2, replica_groups=mesh['ctx'=64,'rep'=4] {'ctx'}, use_global_device_ids=true, to_apply=%region_3.4.clone | all-reduce | flops 6144 | bytes 49152
  704.5 11.6 %reshape.218 = bf16[8192,4,8]{2,1,0:T(4,128)(2,1)} reshape(bf16[64,2,2048]{2,1,0:T(2,128)(2,1)} %all-to-all-done.4) | data formatting | bytes 1048576
  716.1 9.9 %copy.158 = bf16[4,8,64,128]{3,1,2,0:T(8,128)(2,1)S(1)} copy(bf16[4,8,64,128]{1,0,3,2:T(4,128)(2,1)} %bitcast.271) | data formatting | bytes 1048576 | tf_op jit(solution)/shard_map/all_to_all | solution.py:189
  726.0 11.6 %reshape.216 = bf16[8192,4,8]{2,1,0:T(4,128)(2,1)} reshape(bf16[64,2,2048]{2,1,0:T(2,128)(2,1)} %all-to-all-done.5) | data formatting | bytes 1048576
  737.6 10.6 %copy.160 = bf16[4,8,64,128]{3,1,2,0:T(8,128)(2,1)} copy(bf16[4,8,64,128]{1,0,3,2:T(4,128)(2,1)} %bitcast.272) | data formatting | bytes 1048576 | tf_op jit(solution)/shard_map/all_to_all | solution.py:190
  748.2 1.4 copy.130
  749.7 3.4 fusion.55
  753.1 1.3 pad_maximum_fusion
  (157 shorter events, 28.6 us)
Async XLA Ops:
  7.2 24.4 %copy-start = (f32[8,8192]{1,0:T(8,128)S(1)}, f32[8,8192]{1,0:T(8,128)}, u32[]{:S(2)}) copy-start(f32[8,8192]{1,0:T(8,128)} %param.8) | copy-start | bytes 786436
  8.5 50.2 %collective-permute-start.1 = (bf16[1,4,512,2]{3,2,1,0:T(8,128)(2,1)S(1)}, bf16[1,4,512,2]{3,2,1,0:T(8,128)(2,1)}, u32[]{:S(2)}, u32[]{:S(2)}) collective-permute-start(bf16[1,4,512,2]{3,2,1,0:T(8,128)(2,1)S(1)} %slice.170), channel_id=1, source_target_pairs={{0,4},{4,8},{8,12},{12,16},{16,20},{20,24},{24,28},{28,32},{32,36}... | collective-permute-start | bytes 24584 | tf_op jit(solution)/shard_map/ppermute | solution.py:14
  13.3 17.7 %copy-start.43 = (f32[3,4,512,3]{2,1,3,0:T(4,128)S(1)}, f32[3,4,512,3]{2,1,3,0:T(4,128)}, u32[]{:S(2)}) copy-start(f32[3,4,512,3]{2,1,3,0:T(4,128)} %param.6) | copy-start | bytes 221188
  14.5 35.9 %all-to-all-start.1 = ((bf16[4,512,128]{2,0,1:T(4,128)(2,1)}), bf16[4,512,128]{2,0,1:T(4,128)(2,1)S(1)}, u32[]{:S(2)}, u32[]{:S(2)}) async-start(bf16[4,512,128]{2,0,1:T(4,128)(2,1)} %bitcast.261), calls=%async_computation.1 | async-start | bytes 1048576 | tf_op jit(solution)/shard_map/all_to_all | solution.py:168
  28.7 3.8 copy-start.27
  29.5 3.0 copy-start.25
  32.5 24.9 %copy-start.52 = (u32[256]{0:T(256)S(1)}, u32[256]{0:T(256)}, u32[]{:S(2)}) copy-start(u32[256]{0:T(256)} %constant.65) | copy-start | bytes 3076
  50.4 8.3 %copy-start.22 = (bf16[4,512,128]{2,0,1:T(4,128)(2,1)}, bf16[4,512,128]{2,0,1:T(4,128)(2,1)S(1)}, u32[]{:S(2)}) copy-start(bf16[4,512,128]{2,0,1:T(4,128)(2,1)S(1)} %all-to-all-done.1) | copy-start | bytes 1572868
  50.4 25.5 %all-to-all-start = ((bf16[4,512,128]{2,0,1:T(4,128)(2,1)}), bf16[4,512,128]{2,0,1:T(4,128)(2,1)}, u32[]{:S(2)}, u32[]{:S(2)}) async-start(bf16[4,512,128]{2,0,1:T(4,128)(2,1)} %bitcast.262), calls=%async_computation | async-start | bytes 1048576 | tf_op jit(solution)/shard_map/all_to_all | solution.py:167
  56.0 4.4 copy-start.29
  57.4 65.4 %copy-start.31 = (f32[4,8]{1,0:T(4,128)}, f32[4,8]{1,0:T(4,128)S(1)}, u32[]{:S(2)}) copy-start(f32[4,8]{1,0:T(4,128)S(1)} %get-tuple-element.51) | copy-start | bytes 388
  57.4 65.4 %copy-start.33 = (f32[4,8]{1,0:T(4,128)}, f32[4,8]{1,0:T(4,128)S(1)}, u32[]{:S(2)}) copy-start(f32[4,8]{1,0:T(4,128)S(1)} %get-tuple-element.52) | copy-start | bytes 388
  57.4 65.4 %copy-start.35 = (f32[4,8]{1,0:T(4,128)}, f32[4,8]{1,0:T(4,128)S(1)}, u32[]{:S(2)}) copy-start(f32[4,8]{1,0:T(4,128)S(1)} %get-tuple-element.53) | copy-start | bytes 388
  57.4 65.4 %copy-start.37 = (f32[4,8]{1,0:T(4,128)}, f32[4,8]{1,0:T(4,128)S(1)}, u32[]{:S(2)}) copy-start(f32[4,8]{1,0:T(4,128)S(1)} %get-tuple-element.58) | copy-start | bytes 388
  57.4 65.4 %copy-start.39 = (f32[4,8]{1,0:T(4,128)}, f32[4,8]{1,0:T(4,128)S(1)}, u32[]{:S(2)}) copy-start(f32[4,8]{1,0:T(4,128)S(1)} %get-tuple-element.59) | copy-start | bytes 388
  57.4 65.4 %copy-start.41 = (f32[4,8]{1,0:T(4,128)}, f32[4,8]{1,0:T(4,128)S(1)}, u32[]{:S(2)}) copy-start(f32[4,8]{1,0:T(4,128)S(1)} %get-tuple-element.60) | copy-start | bytes 388
  75.9 24.9 %all-to-all-start.3 = ((bf16[4,512,128]{2,0,1:T(4,128)(2,1)}), bf16[4,512,128]{2,0,1:T(4,128)(2,1)}, u32[]{:S(2)}, u32[]{:S(2)}) async-start(bf16[4,512,128]{2,0,1:T(4,128)(2,1)} %copy.131), calls=%async_computation.3 | async-start | bytes 1048576 | tf_op jit(solution)/shard_map/all_to_all | solution.py:169
  81.4 182.8 %reduce-scatter.3.cloned.1.call-start = ((), (), s32[]{:S(2)}) async-start(), calls=%async_computation.7 | async-start | bytes 163840 | tf_op jit(solution)/shard_map/reduce_scatter | solution.py:212
  81.9 2.0 copy-start.23
  85.1 16.9 %copy-start.28 = (f32[128,128]{0,1:T(8,128)S(1)}, f32[128,128]{0,1:T(8,128)}, u32[]{:S(2)}) copy-start(f32[128,128]{0,1:T(8,128)} %copy-done.27) | copy-start | bytes 196612
  86.3 1.0 copy-start.6
  88.4 14.5 %copy-start.26 = (f32[128,128]{0,1:T(8,128)S(1)}, f32[128,128]{0,1:T(8,128)}, u32[]{:S(2)}) copy-start(f32[128,128]{0,1:T(8,128)} %copy-done.25) | copy-start | bytes 196612
  106.5 1.3 copy-start.13
  106.5 1.3 copy-start.15
  107.8 2.9 copy-start.4
  118.7 2.4 copy-start.44
  121.1 1.8 copy-start.7
  121.1 2.0 copy-start.21
  130.4 2.1 copy-start.10
  135.0 1.6 copy-start.5
  135.0 2.2 copy-start.9
  135.0 2.3 copy-start.14
  135.1 2.4 copy-start.16
  144.6 3.2 copy-start.12
  153.2 3.4 copy-start.3
  157.8 1.6 copy-start.2
  163.5 2.5 copy-start.11
  163.5 2.5 copy-start.45
  176.4 16.8 %copy-start.20 = (f32[4,8,8192]{2,1,0:T(8,128)S(1)}, f32[4,8,8192]{2,1,0:T(8,128)}, u32[]{:S(2)}) copy-start(f32[4,8,8192]{2,1,0:T(8,128)} %get-tuple-element.18) | copy-start | bytes 3145732
  176.4 16.8 %copy-start.38 = (f32[4,8]{1,0:T(4,128)S(1)}, f32[4,8]{1,0:T(4,128)}, u32[]{:S(2)}) copy-start(f32[4,8]{1,0:T(4,128)} %copy-done.37) | copy-start | bytes 388
  176.4 16.8 %copy-start.40 = (f32[4,8]{1,0:T(4,128)S(1)}, f32[4,8]{1,0:T(4,128)}, u32[]{:S(2)}) copy-start(f32[4,8]{1,0:T(4,128)} %copy-done.39) | copy-start | bytes 388
  176.4 16.8 %copy-start.42 = (f32[4,8]{1,0:T(4,128)S(1)}, f32[4,8]{1,0:T(4,128)}, u32[]{:S(2)}) copy-start(f32[4,8]{1,0:T(4,128)} %copy-done.41) | copy-start | bytes 388
  187.7 27.9 %all-to-all-start.2 = ((bf16[64,2,2048]{2,1,0:T(2,128)(2,1)}), bf16[64,2,2048]{2,1,0:T(2,128)(2,1)}, u32[]{:S(2)}, u32[]{:S(2)}) async-start(bf16[64,2,2048]{2,1,0:T(2,128)(2,1)} %reshape.219), calls=%async_computation.2 | async-start | bytes 1048576 | tf_op jit(solution)/shard_map/all_to_all | solution.py:188
  204.3 24.4 %copy-start.19 = (f32[4,8,8192]{2,1,0:T(8,128)S(1)}, f32[4,8,8192]{2,1,0:T(8,128)}, u32[]{:S(2)}) copy-start(f32[4,8,8192]{2,1,0:T(8,128)} %get-tuple-element.37) | copy-start | bytes 3145732
  204.3 24.4 %copy-start.32 = (f32[4,8]{1,0:T(4,128)S(1)}, f32[4,8]{1,0:T(4,128)}, u32[]{:S(2)}) copy-start(f32[4,8]{1,0:T(4,128)} %copy-done.31) | copy-start | bytes 388
  204.3 24.4 %copy-start.34 = (f32[4,8]{1,0:T(4,128)S(1)}, f32[4,8]{1,0:T(4,128)}, u32[]{:S(2)}) copy-start(f32[4,8]{1,0:T(4,128)} %copy-done.33) | copy-start | bytes 388
  204.3 24.4 %copy-start.36 = (f32[4,8]{1,0:T(4,128)S(1)}, f32[4,8]{1,0:T(4,128)}, u32[]{:S(2)}) copy-start(f32[4,8]{1,0:T(4,128)} %copy-done.35) | copy-start | bytes 388
  215.6 35.4 %all-to-all-start.4 = ((bf16[64,2,2048]{2,1,0:T(2,128)(2,1)}), bf16[64,2,2048]{2,1,0:T(2,128)(2,1)}, u32[]{:S(2)}, u32[]{:S(2)}) async-start(bf16[64,2,2048]{2,1,0:T(2,128)(2,1)} %reshape.217), calls=%async_computation.4 | async-start | bytes 1048576 | tf_op jit(solution)/shard_map/all_to_all | solution.py:189
  239.7 11.2 %copy-start.49 = (f32[4,8]{1,0:T(4,128)S(1)}, f32[4,8]{1,0:T(4,128)}, u32[]{:S(2)}) copy-start(f32[4,8]{1,0:T(4,128)} %get-tuple-element.11) | copy-start | bytes 388
  239.7 11.2 %copy-start.50 = (f32[4,8]{1,0:T(4,128)S(1)}, f32[4,8]{1,0:T(4,128)}, u32[]{:S(2)}) copy-start(f32[4,8]{1,0:T(4,128)} %get-tuple-element.12) | copy-start | bytes 388
  239.7 11.2 %copy-start.51 = (f32[4,8]{1,0:T(4,128)S(1)}, f32[4,8]{1,0:T(4,128)}, u32[]{:S(2)}) copy-start(f32[4,8]{1,0:T(4,128)} %get-tuple-element.15) | copy-start | bytes 388
  239.7 24.4 %copy-start.46 = (f32[4,8]{1,0:T(4,128)S(1)}, f32[4,8]{1,0:T(4,128)}, u32[]{:S(2)}) copy-start(f32[4,8]{1,0:T(4,128)} %get-tuple-element.34) | copy-start | bytes 388
  239.7 24.4 %copy-start.47 = (f32[4,8]{1,0:T(4,128)S(1)}, f32[4,8]{1,0:T(4,128)}, u32[]{:S(2)}) copy-start(f32[4,8]{1,0:T(4,128)} %get-tuple-element.35) | copy-start | bytes 388
  239.7 24.4 %copy-start.48 = (f32[4,8]{1,0:T(4,128)S(1)}, f32[4,8]{1,0:T(4,128)}, u32[]{:S(2)}) copy-start(f32[4,8]{1,0:T(4,128)} %get-tuple-element.36) | copy-start | bytes 388
  251.0 475.0 %all-to-all-start.5 = ((bf16[64,2,2048]{2,1,0:T(2,128)(2,1)}), bf16[64,2,2048]{2,1,0:T(2,128)(2,1)}, u32[]{:S(2)}, u32[]{:S(2)}) async-start(bf16[64,2,2048]{2,1,0:T(2,128)(2,1)} %reshape.215), calls=%async_computation.5 | async-start | bytes 1048576 | tf_op jit(solution)/shard_map/all_to_all | solution.py:190
  286.9 1.0 copy-start.17
  291.9 456.3 %collective-permute-start = (f32[1,4,512,2]{2,1,3,0:T(4,128)S(1)}, f32[1,4,512,2]{2,1,3,0:T(4,128)S(1)}, u32[]{:S(2)}, u32[]{:S(2)}) collective-permute-start(f32[1,4,512,2]{2,1,3,0:T(4,128)S(1)} %copy.129), channel_id=1, source_target_pairs={{4,0},{8,4},{12,8},{16,12},{20,16},{24,20},{28,24},{32,28},{36,32}... | collective-permute-start | bytes 49160 | tf_op jit(solution)/shard_map/ppermute | solution.py:14
  737.6 12.0 %copy-start.8 = (f32[1,4,512,128]{3,2,1,0:T(8,128)S(1)}, f32[1,4,512,128]{3,2,1,0:T(8,128)}, u32[]{:S(2)}) copy-start(f32[1,4,512,128]{3,2,1,0:T(8,128)} %get-tuple-element.17) | copy-start | bytes 3145732
  737.6 12.0 %copy-start.18 = (bf16[4,512,128]{2,1,0:T(8,128)(2,1)S(1)}, bf16[4,512,128]{2,1,0:T(8,128)(2,1)}, u32[]{:S(2)}) copy-start(bf16[4,512,128]{2,1,0:T(8,128)(2,1)} %param.9) | copy-start | bytes 1572868
  737.6 12.0 %copy-start.30 = (f32[4,512]{1,0:T(4,128)S(1)}, f32[4,512]{1,0:T(4,128)}, u32[]{:S(2)}) copy-start(f32[4,512]{1,0:T(4,128)} %get-tuple-element.50) | copy-start | bytes 24580
  749.6 3.5 copy-start.24
  749.6 4.8 copy-start.1
Sparse Core Ops, SparseCore 0:
  153.3 15.4 reduce-scatter.2
where the time goes:
time: 772 us; the launch traced here: 761 us
  blocking collectives  411 us (53%)
  local copies, waits for them, and re-layouts  151 us (20%)
  starting transfers between devices  61 us (8%)
  matrix products  48.5 us (6%)
  waiting for transfers between devices  41.5 us (5%)
  other arithmetic  33.3 us (4%)
  between operations  15.8 us (2%)
    unnamed x1, blocking collectives  411 us
    unnamed x119, local copies, waits for them, and re-layouts  76.5 us
    all_to_all x1, waiting for transfers between devices, per_device(): lax.all_to_all(features[2], 'ctx', split_axis=1, concat_axis=2, tiled=True)  17.2 us
  transfers between devices with their start and end apart: 9, of which 3 were waited for; matrix products, arithmetic and copies ran while one was open for 22% of the time, Pallas kernels for 0%

commit v1 on v0

v1 whole, which is shorter than its diff:
```python
import functools

import jax
import jax.numpy as jnp
from jax import lax
from jax.experimental import pallas as pl
from jax.experimental.pallas import tpu as pltpu
from jax.sharding import PartitionSpec as P

MESH = pl.DeviceIdType.MESH
F32 = jnp.float32
BF16 = jnp.bfloat16

SHARDS = 64
REPS = 4
LANES = 128
CHUNKS = 2
QUAD = 4
GROUP = 8
LAGS = 64


def lane_ids():
    return lax.broadcasted_iota(jnp.int32, (8, LANES), 1)


def row_ids():
    return lax.broadcasted_iota(jnp.int32, (8, LANES), 0)


def swap_halves(first, second):
    upper = row_ids() < QUAD
    return (
        jnp.where(upper, first, pltpu.roll(second, QUAD, 0)),
        jnp.where(upper, pltpu.roll(first, QUAD, 0), second),
    )


def flip_matrix():
    rows = lax.broadcasted_iota(jnp.int32, (LANES, LANES), 0)
    cols = lax.broadcasted_iota(jnp.int32, (LANES, LANES), 1)
    return jnp.where(rows + cols == LANES - 1, 1.0, 0.0).astype(BF16)


def column(tile, lane):
    return jnp.broadcast_to(tile[:, lane : lane + 1], (8, LANES))


def kernel(
    feat, cot, taps, skip, filt,
    d_feat, d_short, d_skip, d_filt,
    sig, mixed, wts, tcol, strip, base, front, front_in,
    send_in, recv_in, send_out, recv_out,
    spread, prod_nat, grad_nat, xs, conv, merged,
    shifted, prod_t, cross, low, high, lagrow, lag_send, lag_recv,
    grads, back, back_in, tap_send, tap_recv,
    front_sem, in_sem, out_sem, back_sem, tap_sem, lag_sem,
):
    me = lax.axis_index("ctx")
    rep = lax.axis_index("rep")
    lane = lane_ids()

    barrier = pltpu.get_barrier_semaphore()

    def greet(k, _):
        pl.semaphore_signal(
            barrier, inc=1, device_id=(lax.rem(me + k, SHARDS), rep), device_id_type=MESH
        )
        return 0

    lax.fori_loop(1, SHARDS, greet, 0)
    for k in range(1, REPS):
        pl.semaphore_signal(
            barrier, inc=1, device_id=(me, lax.rem(rep + k, REPS)), device_id_type=MESH
        )

    def arrange(step, packed):
        packed = list(packed)
        for half in range(4):
            pair = step * 4 + half
            rows = pl.ds(pl.multiple_of(pair * 16, 16), 16)
            for j in range(4):
                wide = []
                for g in range(4):
                    block = feat[j, g, rows, :] if j < 3 else cot[g, rows, :]
                    wide.append(block.astype(F32))
                for u in range(2):
                    shard = pair * 2 + u
                    for gp in range(2):
                        tiles = swap_halves(
                            wide[2 * gp][8 * u : 8 * u + 8], wide[2 * gp + 1][8 * u : 8 * u + 8]
                        )
                        for c in range(CHUNKS):
                            sig[j, c, shard, 8 * gp : 8 * gp + 8, :] = tiles[c]
                            if j < 3:
                                at = (c * 3 + j) * 2 + gp
                                moved = pltpu.roll(tiles[c], lax.rem(2 * shard + 2, LANES), 1)
                                packed[at] = jnp.where(lane // 2 == shard, moved, packed[at])
        return tuple(packed)

    zero = jnp.zeros((8, LANES), F32)
    packed = lax.fori_loop(0, SHARDS // 8, arrange, (zero,) * 12)
    for at in range(12):
        front[8 * at : 8 * at + 8, :] = packed[at]

    @pl.when(me == 0)
    def _():
        front_in[...] = jnp.zeros(front_in.shape, F32)

    @pl.when(me == SHARDS - 1)
    def _():
        back_in[...] = jnp.zeros(back_in.shape, F32)

    pl.semaphore_wait(barrier, SHARDS - 1 + REPS - 1)

    def front_copy():
        return pltpu.make_async_remote_copy(
            src_ref=front, dst_ref=front_in, send_sem=front_sem.at[0], recv_sem=front_sem.at[1],
            device_id=(lax.rem(me + 1, SHARDS), rep), device_id_type=MESH,
        )

    @pl.when(me < SHARDS - 1)
    def _():
        front_copy().start()

    for part in range(4):
        cols = slice(part * LANES, (part + 1) * LANES)
        tcol[cols, :] = jnp.concatenate(
            [taps[:, cols], jnp.zeros((LANES - 40, LANES), F32)], axis=0
        ).T

    def arrange_taps(step, _):
        for u in range(8):
            shard = step * 8 + u
            tile = tcol[pl.ds(pl.multiple_of(shard * 8, 8), 8), :]
            for gp in range(2):
                first = tile if gp == 0 else pltpu.roll(tile, LANES - 18 * gp, 1)
                second = pltpu.roll(tile, LANES - 18 * gp - 9, 1)
                both = swap_halves(first, second)
                for c in range(CHUNKS):
                    wts[c, shard, 8 * gp : 8 * gp + 8, :] = both[c]
        return 0

    lax.fori_loop(0, SHARDS // 8, arrange_taps, 0)

    for q in range(QUAD):
        for u in range(2):
            xs[q, u, 0:256, :] = jnp.zeros((256, 256), BF16)
        for e in range(2):
            for k in range(4):
                shifted[q, e, k, 128:256, :] = jnp.zeros((128, LANES), BF16)
        high[q, LAGS] = zero
    for e in range(2):
        grad_nat[e, 512:576, :] = jnp.zeros((64, LANES), F32)

    @pl.when(me > 0)
    def _():
        front_copy().wait_recv()

    @pl.when(me < SHARDS - 1)
    def _():
        front_copy().wait_send()

    def block_copy(src, dst, sems, c, peer):
        return pltpu.make_async_remote_copy(
            src_ref=src.at[c, peer], dst_ref=dst.at[c, me], send_sem=sems.at[0, c],
            recv_sem=sems.at[1, c], device_id=(peer, rep), device_id_type=MESH,
        )

    def all_copies(src, dst, sems, c):
        others = pl.ds(0, SHARDS - 1)
        return pltpu.make_async_remote_copy(
            src_ref=src.at[c, others], dst_ref=dst.at[c, others], send_sem=sems.at[0, c],
            recv_sem=sems.at[1, c], device_id=(lax.rem(me + 1, SHARDS), rep), device_id_type=MESH,
        )

    def send_all(src, dst, sems, c):
        def one(k, _):
            block_copy(src, dst, sems, c, lax.rem(me + k, SHARDS)).start()
            return 0

        lax.fori_loop(1, SHARDS, one, 0)
        dst[c, me] = src[c, me]

    def short_conv(c, step, _):
        for u in range(GROUP):
            shard = lax.rem(me + step * GROUP + u, SHARDS)
            made = []
            for gp in range(2):
                rows = slice(8 * gp, 8 * gp + 8)
                weight = wts[c, shard, rows, :]
                mix = []
                for j in range(3):
                    here = sig[j, c, shard, rows, :]
                    at = (c * 3 + j) * 2 + gp
                    before = pltpu.roll(front_in[8 * at : 8 * at + 8, :], 126 - 2 * shard, 1)
                    one = pltpu.roll(jnp.where(lane == 127, before, here), 1, 1)
                    two = pltpu.roll(jnp.where(lane >= 126, before, here), 2, 1)
                    mix.append(
                        column(weight, 3 * j) * here
                        + column(weight, 3 * j + 1) * one
                        + column(weight, 3 * j + 2) * two
                    )
                mixed[0, c, shard, rows, :] = mix[1]
                mixed[1, c, shard, rows, :] = mix[2]
                made.append((mix[1] * mix[2], sig[3, c, shard, rows, :] * mix[0]))
            for a in range(2):
                send_in[c, shard, 16 * a : 16 * a + 16, :] = jnp.concatenate(
                    [made[0][a], made[1][a]], axis=0
                ).astype(BF16)
        for u in range(GROUP):
            shard = lax.rem(me + step * GROUP + u, SHARDS)

            @pl.when(shard != me)
            def _():
                block_copy(send_in, recv_in, in_sem, c, shard).start()

        return 0

    for c in range(CHUNKS):
        lax.fori_loop(0, SHARDS // GROUP, functools.partial(short_conv, c), 0)
        recv_in[c, me] = send_in[c, me]

    strip[:, :, 0:LANES] = jnp.zeros((8, LANES, LANES), BF16)
    base[:, 0:LANES] = zero

    def make_strip(f, _):
        row = filt[pl.ds(f, 1), :]
        for part in range(8):
            cols = slice(LANES + part * 1024, LANES + part * 1024 + 1024)
            base[:, cols] = jnp.broadcast_to(row[:, part * 1024 : part * 1024 + 1024], (8, 1024))
        for part in reversed(range(8)):
            wide = base[:, part * 1024 : part * 1024 + 1152]
            base[:, LANES + part * 1024 : LANES + part * 1024 + 1024] = pltpu.roll(
                wide, 0, 1, stride=1, stride_axis=0
            )[:, LANES:]
        for part in range(8):
            wide = base[:, part * 1024 : part * 1024 + 1152]
            for k in range(8):
                upper = wide if k == 0 else pltpu.roll(wide, 16 * k, 1)
                lower = pltpu.roll(wide, 16 * k + 8, 1)
                strip[f, 16 * k : 16 * k + 16, LANES + part * 1024 : LANES + part * 1024 + 1024] = (
                    jnp.concatenate([upper[:, LANES:], lower[:, LANES:]], axis=0).astype(BF16)
                )
        return 0

    lax.fori_loop(0, 8, make_strip, 0)

    flip = flip_matrix()
    sign_row = lax.broadcasted_iota(jnp.int32, (8, 256), 0) % 4

    def unpack(c, step, total):
        back_rows = jnp.concatenate(
            [recv_in[c, step * 8 + u, 16:32, :] for u in range(8)], axis=0
        )
        turned = jnp.dot(back_rows, flip, preferred_element_type=F32)
        for u in range(8):
            shard = step * 8 + u
            place = step * 4 + u // 2
            e = u % 2
            product = recv_in[c, shard, 0:16, :].astype(F32)
            gated = recv_in[c, shard, 16:32, :].astype(F32)
            total = total + product * gated
            spread[e, pl.ds(pl.multiple_of(place * 32, 32), 16), :] = product
            prod_nat[e, pl.ds(pl.multiple_of(place * 16, 16), 16), :] = product
            reverse = turned[16 * u : 16 * u + 16]
            mirror = 31 - place
            spread[1 - e, pl.ds(pl.multiple_of(mirror * 32 + 16, 16), 16), :] = reverse
            grad_nat[e, pl.ds(pl.multiple_of(place * 16, 16), 16), :] = reverse
        return total

    def long_conv(c, q, _):
        f = QUAD * c + q
        for group in range(4):
            skip_rows = 64 * group
            acc = jnp.zeros((256 - skip_rows, 256), F32)
            for lag in range(8 * group, 8 * group + 8):
                even = lag - lag % 2
                lhs = xs[q, lag % 2, 256 + skip_rows - 8 * even : 512 - 8 * even, :]
                at = LANES + 256 * lag
                rhs = jnp.concatenate(
                    [strip[f, :, at : at + 256], strip[f, :, at - LANES : at + LANES]], axis=0
                )
                acc = acc + jnp.dot(lhs, rhs, preferred_element_type=F32)
            if group == 0:
                conv[q] = acc
            else:
                conv[q, skip_rows:256, :] += acc
        gain = jnp.where(
            sign_row == 0,
            skip[0, f],
            jnp.where(sign_row == 1, skip[1, f], jnp.where(sign_row == 2, skip[2, f], skip[3, f])),
        )
        for part in range(4):
            rows = slice(64 * part, 64 * part + 64)
            own = xs[q, 0, 256 + 64 * part : 320 + 64 * part, :].astype(F32)
            conv[q, rows, :] += own * jnp.concatenate([gain] * 8, axis=0)
        return 0

    def pack(c, step, _):
        turned = jnp.concatenate(
            [
                merged[u % 2, pl.ds(pl.multiple_of((step * 4 + u // 2) * 32 + 16, 16), 16), :]
                for u in range(8)
            ],
            axis=0,
        ).astype(BF16)
        turned = jnp.dot(turned, flip, preferred_element_type=F32).astype(BF16)
        for u in range(8):
            shard = step * 8 + u
            place = step * 4 + u // 2
            send_out[c, shard, 0:16, :] = merged[
                u % 2, pl.ds(pl.multiple_of(place * 32, 32), 16), :
            ].astype(BF16)
            send_out[c, SHARDS - 1 - shard, 16:32, :] = turned[16 * u : 16 * u + 16]
        return 0

    def owner_conv(c):
        all_copies(send_in, recv_in, in_sem, c).wait_recv()
        total = lax.fori_loop(0, 8, functools.partial(unpack, c), jnp.zeros((16, LANES), F32))
        d_skip[16 * c : 16 * c + 16, :] = jnp.broadcast_to(
            jnp.sum(total, axis=1, keepdims=True), (16, LANES)
        )
        for q in range(QUAD):
            tile = jnp.concatenate(
                [spread[e, pl.ds(q, 256, stride=4), :] for e in range(2)], axis=1
            )
            xs[q, 0, 256:512, :] = tile.astype(BF16)
            xs[q, 1, 256:512, :] = jnp.concatenate(
                [jnp.zeros((8, 256), F32), tile[0:248]], axis=0
            ).astype(BF16)
        lax.fori_loop(0, QUAD, functools.partial(long_conv, c), 0)
        for q in range(QUAD):
            for e in range(2):
                merged[e, pl.ds(q, 256, stride=4), :] = conv[q, :, LANES * e : LANES * e + LANES]
        lax.fori_loop(0, 8, functools.partial(pack, c), 0)
        send_all(send_out, recv_out, out_sem, c)

    def cross_dots(q, m, slot):
        for pair in range(4):
            sides = []
            for odd in range(2):
                lag = 2 * pair + odd
                half = pair
                parts = []
                for e in range(2):
                    carry = half + (1 if e == 1 and odd == 1 else 0)
                    at = pl.multiple_of(16 * m + 16 * (carry // 4), 16)
                    parts.append(shifted[q, (e + odd) % 2, carry % 4, pl.ds(at, 128), :])
                sides.append(jnp.concatenate(parts, axis=0))
            cross[slot, pair] = jnp.dot(
                prod_t[q], jnp.concatenate(sides, axis=1), preferred_element_type=F32
            )

    def diagonals(q, m, slot):
        for lag in range(8):
            cols = slice((lag % 2) * LANES, (lag % 2) * LANES + LANES)
            total = cross[slot, lag // 2, 0:8, cols]
            kept = total
            for k in range(1, 16):
                moved = pltpu.roll(cross[slot, lag // 2, 8 * k : 8 * k + 8, cols], 8 * k, 1)
                total = total + moved
                kept = kept + jnp.where(lane >= 8 * k, moved, 0.0)
            low[q, 8 * m + lag] = kept
            high[q, 8 * m + lag] = total - kept

    def owner_lags(c):
        for q in range(QUAD):
            for e in range(2):
                prod_t[q, :, LANES * e : LANES * e + LANES] = (
                    prod_nat[e, pl.ds(q, 128, stride=4), :].T.astype(BF16)
                )
                for k in range(4):
                    shifted[q, e, k, 0:128, :] = grad_nat[
                        e, pl.ds(q + 16 * k, 128, stride=4), :
                    ].astype(BF16)
        cross_dots(0, 0, 0)

        def two(step, _):
            q = step // 4
            m = 2 * (step % 4)
            cross_dots(q, m + 1, 1)
            diagonals(q, m, 0)
            later = jnp.minimum(step + 1, 15)
            cross_dots(later // 4, 2 * (later % 4), 0)
            diagonals(q, m + 1, 1)
            return 0

        lax.fori_loop(0, 16, two, 0)

        def turn(step, _):
            q = step // 4
            first = 16 * (step % 4)
            rolled = []
            for k in range(17):
                at = jnp.minimum(first + k, LAGS - 1)
                tile = low[q, at] + high[q, at + 1]
                rolled.append(pltpu.roll(tile, 0, 1, stride=1, stride_axis=0))
            rolled[16] = jnp.where(first == 48, 0.0, rolled[16])
            rows = [
                jnp.sum(jnp.where(lane >= row_ids(), rolled[k], rolled[k + 1]), axis=0, keepdims=True)
                for k in range(16)
            ]
            lagrow[q, step % 4] = jnp.concatenate(rows, axis=0)
            return 0

        lax.fori_loop(0, 16, turn, 0)
        for q in range(QUAD):
            turned = jnp.dot(
                jnp.concatenate([lagrow[q, r] for r in range(4)], axis=0).astype(BF16),
                flip,
                preferred_element_type=F32,
            ).astype(BF16)
            for r in range(REPS):
                lag_send[r, QUAD * c + q] = turned[16 * r : 16 * r + 16]

    owner_conv(0)
    owner_lags(0)
    owner_conv(1)
    owner_lags(1)

    def lag_copy(peer):
        return pltpu.make_async_remote_copy(
            src_ref=lag_send.at[peer], dst_ref=lag_recv.at[rep], send_sem=lag_sem.at[0],
            recv_sem=lag_sem.at[1], device_id=(me, peer), device_id_type=MESH,
        )

    for k in range(1, REPS):
        lag_copy(lax.rem(rep + k, REPS)).start()
    lag_recv[rep] = lag_send[rep]

    def make_grads(c, step, packed):
        packed = list(packed)
        for u in range(GROUP):
            shard = step * GROUP + u
            conv_rows = recv_out[c, shard, 0:16, :].astype(F32)
            grad_rows = recv_out[c, shard, 16:32, :].astype(F32)
            for gp in range(2):
                rows = slice(8 * gp, 8 * gp + 8)
                value = grad_rows[rows]
                three = (
                    sig[3, c, shard, rows, :] * conv_rows[rows],
                    value * mixed[1, c, shard, rows, :],
                    value * mixed[0, c, shard, rows, :],
                )
                for j in range(3):
                    grads[c, j, shard, rows, :] = three[j]
                    moved = pltpu.roll(three[j], 2 * shard, 1)
                    packed[2 * j + gp] = jnp.where(lane // 2 == shard, moved, packed[2 * j + gp])
        return tuple(packed)

    def back_copy(c):
        return pltpu.make_async_remote_copy(
            src_ref=back.at[c], dst_ref=back_in.at[c], send_sem=back_sem.at[0, c],
            recv_sem=back_sem.at[1, c],
            device_id=(lax.rem(me + SHARDS - 1, SHARDS), rep), device_id_type=MESH,
        )

    def post_first(c):
        all_copies(send_out, recv_out, out_sem, c).wait_recv()
        packed = lax.fori_loop(
            0, SHARDS // GROUP, functools.partial(make_grads, c), (zero,) * 6
        )
        for at in range(6):
            back[c, 8 * at : 8 * at + 8, :] = packed[at]

        @pl.when(me > 0)
        def _():
            back_copy(c).start()

    def short_back(c, step, _):
        for u in range(GROUP):
            shard = step * GROUP + u
            sums = tap_send[shard] if c == 1 else zero
            for gp in range(2):
                rows = slice(8 * gp, 8 * gp + 8)
                weight = wts[c, shard, rows, :]
                for j in range(3):
                    here = grads[c, j, shard, rows, :]
                    at = 2 * j + gp
                    after = pltpu.roll(
                        back_in[c, 8 * at : 8 * at + 8, :], lax.rem(LANES - 2 * shard, LANES), 1
                    )
                    one = pltpu.roll(jnp.where(lane == 0, after, here), LANES - 1, 1)
                    two = pltpu.roll(jnp.where(lane < 2, after, here), LANES - 2, 1)
                    grads[c, j, shard, rows, :] = (
                        column(weight, 3 * j) * here
                        + column(weight, 3 * j + 1) * one
                        + column(weight, 3 * j + 2) * two
                    )
                    signal = sig[j, c, shard, rows, :]
                    for i, moved in enumerate((here, one, two)):
                        share = jnp.sum(moved * signal, axis=1, keepdims=True)
                        sums = jnp.where(lane == c * 18 + gp * 9 + 3 * j + i, share, sums)
            tap_send[shard] = sums
        return 0

    def post_second(c):
        @pl.when(me < SHARDS - 1)
        def _():
            back_copy(c).wait_recv()

        lax.fori_loop(0, SHARDS // GROUP, functools.partial(short_back, c), 0)

    post_first(0)
    post_first(1)
    post_second(0)
    post_second(1)

    def tap_copy(peer):
        return pltpu.make_async_remote_copy(
            src_ref=tap_send.at[peer], dst_ref=tap_recv.at[me], send_sem=tap_sem.at[0],
            recv_sem=tap_sem.at[1], device_id=(peer, rep), device_id_type=MESH,
        )

    def send_taps(k, _):
        tap_copy(lax.rem(me + k, SHARDS)).start()
        return 0

    lax.fori_loop(1, SHARDS, send_taps, 0)
    tap_recv[me] = tap_send[me]

    def put_back(step, _):
        for half in range(4):
            pair = step * 4 + half
            rows = pl.ds(pl.multiple_of(pair * 16, 16), 16)
            for j in range(3):
                for gp in range(2):
                    tiles = [
                        swap_halves(
                            grads[0, j, pair * 2 + u, 8 * gp : 8 * gp + 8, :],
                            grads[1, j, pair * 2 + u, 8 * gp : 8 * gp + 8, :],
                        )
                        for u in range(2)
                    ]
                    for g in range(2):
                        d_feat[j, 2 * gp + g, rows, :] = jnp.concatenate(
                            [tiles[0][g], tiles[1][g]], axis=0
                        ).astype(BF16)
        return 0

    lax.fori_loop(0, SHARDS // 8, put_back, 0)

    lag_all = pltpu.make_async_remote_copy(
        src_ref=lag_send.at[pl.ds(0, REPS - 1)], dst_ref=lag_recv.at[pl.ds(0, REPS - 1)],
        send_sem=lag_sem.at[0], recv_sem=lag_sem.at[1],
        device_id=(me, lax.rem(rep + 1, REPS)), device_id_type=MESH,
    )
    lag_all.wait_recv()
    for f in range(8):
        d_filt[f] = (
            lag_recv[0, f].astype(F32)
            + lag_recv[1, f].astype(F32)
            + lag_recv[2, f].astype(F32)
            + lag_recv[3, f].astype(F32)
        )

    tap_all = pltpu.make_async_remote_copy(
        src_ref=tap_send.at[pl.ds(0, SHARDS - 1)], dst_ref=tap_recv.at[pl.ds(0, SHARDS - 1)],
        send_sem=tap_sem.at[0], recv_sem=tap_sem.at[1],
        device_id=(lax.rem(me + 1, SHARDS), rep), device_id_type=MESH,
    )
    tap_all.wait_recv()
    d_short[...] = jnp.sum(tap_recv[...], axis=0)

    for c in range(CHUNKS):
        all_copies(send_in, recv_in, in_sem, c).wait_send()
        all_copies(send_out, recv_out, out_sem, c).wait_send()

        @pl.when(me > 0)
        def _():
            back_copy(c).wait_send()

    lag_all.wait_send()
    tap_all.wait_send()


def per_device(features, short_taps, skip_gain, filters, cotangent):
    tap_rows = jnp.transpose(short_taps, (1, 0, 3, 2)).reshape(36, 512)
    tap_rows = jnp.pad(tap_rows, ((0, 4), (0, 0)))
    vmem = pl.BlockSpec(memory_space=pltpu.VMEM)
    message = pltpu.VMEM((CHUNKS, SHARDS, 32, LANES), BF16)
    d_feat, d_short, d_skip, d_filt = pl.pallas_call(
        kernel,
        out_shape=(
            jax.ShapeDtypeStruct((3, 4, 512, LANES), BF16),
            jax.ShapeDtypeStruct((8, LANES), F32),
            jax.ShapeDtypeStruct((32, LANES), F32),
            jax.ShapeDtypeStruct((8, 16, LANES), F32),
        ),
        in_specs=[vmem, vmem, vmem, pl.BlockSpec(memory_space=pltpu.SMEM), vmem],
        out_specs=(vmem,) * 4,
        scratch_shapes=[
            pltpu.VMEM((4, CHUNKS, SHARDS, 16, LANES), F32),
            pltpu.VMEM((2, CHUNKS, SHARDS, 16, LANES), F32),
            pltpu.VMEM((CHUNKS, SHARDS, 16, LANES), F32),
            pltpu.VMEM((512, LANES), F32),
            pltpu.VMEM((8, LANES, LANES + 8192), BF16),
            pltpu.VMEM((8, LANES + 8192), F32),
            pltpu.VMEM((96, LANES), F32),
            pltpu.VMEM((96, LANES), F32),
            message, message, message, message,
            pltpu.VMEM((2, 1024, LANES), F32),
            pltpu.VMEM((2, 512, LANES), F32),
            pltpu.VMEM((2, 576, LANES), F32),
            pltpu.VMEM((QUAD, 2, 512, 256), BF16),
            pltpu.VMEM((QUAD, 256, 256), F32),
            pltpu.VMEM((2, 1024, LANES), F32),
            pltpu.VMEM((QUAD, 2, 4, 256, LANES), BF16),
            pltpu.VMEM((QUAD, LANES, 256), BF16),
            pltpu.VMEM((2, 4, LANES, 256), F32),
            pltpu.VMEM((QUAD, LAGS, 8, LANES), F32),
            pltpu.VMEM((QUAD, LAGS + 1, 8, LANES), F32),
            pltpu.VMEM((QUAD, 4, 16, LANES), F32),
            pltpu.VMEM((REPS, 8, 16, LANES), BF16),
            pltpu.VMEM((REPS, 8, 16, LANES), BF16),
            pltpu.VMEM((CHUNKS, 3, SHARDS, 16, LANES), F32),
            pltpu.VMEM((CHUNKS, 48, LANES), F32),
            pltpu.VMEM((CHUNKS, 48, LANES), F32),
            pltpu.VMEM((SHARDS, 8, LANES), F32),
            pltpu.VMEM((SHARDS, 8, LANES), F32),
            pltpu.SemaphoreType.DMA((2,)),
            pltpu.SemaphoreType.DMA((2, CHUNKS)),
            pltpu.SemaphoreType.DMA((2, CHUNKS)),
            pltpu.SemaphoreType.DMA((2, CHUNKS)),
            pltpu.SemaphoreType.DMA((2,)),
            pltpu.SemaphoreType.DMA((2,)),
        ],
        compiler_params=pltpu.CompilerParams(
            collective_id=0, has_side_effects=True, vmem_limit_bytes=60 * 2**20
        ),
    )(features, cotangent, tap_rows, skip_gain, filters)
    short = d_short[:, :36].reshape(2, 4, 2, 2, 3, 3)
    short = jnp.transpose(short, (4, 3, 0, 2, 1, 5)).reshape(3, 4, 8, 3)
    skips = jnp.transpose(d_skip[:, 0].reshape(2, 4, 4), (1, 0, 2)).reshape(4, 8)
    return (d_feat, short, skips, d_filt.reshape(8, 2048))


def solution(mesh):
    placed = (
        P(None, "rep", None, "ctx"),
        P(None, "rep", None, None),
        P("rep", "ctx"),
        P("ctx", None),
        P("rep", None, "ctx"),
    )
    return jax.shard_map(
        per_device,
        mesh=mesh,
        in_specs=placed,
        out_specs=(
            P(None, "rep", None, "ctx"),
            P(None, "rep", "ctx", None),
            P("rep", "ctx"),
            P("ctx", "rep"),
        ),
        check_vma=False,
    )
```

time: 772 us -> 190 us (0.25)
  the two profiles are of different devices: /device:TPU:32 before, /device:TPU:1 now
where the time goes in v1:
time: 190 us
  Pallas kernels  180 us (95%)
  local copies, waits for them, and re-layouts  8.93 us (5%)
    pallas_call x1, Pallas kernels, per_device(): pl.pallas_call(kernel, out_shape=(jax.ShapeDtypeStruct((3, 4, 512, LANES)...  180 us
    unnamed x2, local copies, waits for them, and re-layouts  4.14 us

profile of v1, /device:TPU:1, one launch (start us, length us, event | category | flops | bytes accessed | tf_op | source)
XLA Modules:
  0.0 190.0 jit_solution(9192058545879807905)
XLA Ops:
  0.6 0.9 copy.15
  1.6 0.6 pad.4.taps
  2.3 180.4 %shard_map.84 = (bf16[3,4,512,128]{3,2,1,0:T(8,128)(2,1)}, f32[8,128]{1,0:T(8,128)}, f32[32,128]{1,0:T(8,128)}, f32[8,16,128]{2,1,0:T(8,128)}) custom-call(bf16[3,4,512,128]{3,2,1,0:T(8,128)(2,1)} %feat.1, bf16[4,512,128]{2,1,0:T(8,128)(2,1)} %cot.1, f32[40,512]{1,0:T(8,128)} %pad.4.taps, f32[4,8]{1,0:T(4,128)} %skip.1, f32[8,8192]{1,0:T(8,128)} %filt.1), custom_call_target="tpu_custom_call" | custom-call | tf_op jit(solution)/shard_map/pallas_call | solution.py:583
  182.6 0.8 slice_reduce_fusion
  183.5 0.1 reshape_squeeze.3
  183.6 0.7 reshape.26
  184.2 0.8 copy.16
  185.0 0.1 reshape.24
  185.1 0.7 reshape.25
  185.8 1.5 copy.21
  187.3 2.7 %copy.23 = bf16[3,4,512,128]{3,2,1,0:T(8,128)(2,1)} copy(bf16[3,4,512,128]{3,2,1,0:T(8,128)(2,1)} %get-tuple-element.16) | data formatting | bytes 3145728
  (3 shorter events, 0.1 us)

commit v2 on v1

--- a/solution.py
+++ b/solution.py
@@ -42,18 +42,36 @@
     return jnp.where(rows + cols == LANES - 1, 1.0, 0.0).astype(BF16)
 
 
-def column(tile, lane):
-    return jnp.broadcast_to(tile[:, lane : lane + 1], (8, LANES))
+def ids(rows, cols):
+    shape = (rows, cols)
+    return (
+        lax.broadcasted_iota(jnp.int32, shape, 0),
+        lax.broadcasted_iota(jnp.int32, shape, 1),
+    )
+
+
+def ones_where(condition):
+    return jnp.where(condition, 1.0, 0.0).astype(BF16)
+
+
+def halves(wide):
+    high = wide.astype(BF16)
+    return jnp.concatenate([high, (wide - high.astype(F32)).astype(BF16)], axis=1)
+
+
+def product_of(left, right):
+    return jnp.dot(left, right, preferred_element_type=F32)
 
 
 def kernel(
     feat, cot, taps, skip, filt,
     d_feat, d_short, d_skip, d_filt,
-    sig, mixed, wts, tcol, strip, base, front, front_in,
+    sig, mixed, wts, tcol, strip, base, front, front_in, halo,
+    m_early, m_col, m_late, m_next, m_first, m_sum,
     send_in, recv_in, send_out, recv_out,
     spread, prod_nat, grad_nat, xs, conv, merged,
     shifted, prod_t, cross, low, high, lagrow, lag_send, lag_recv,
-    grads, back, back_in, tap_send, tap_recv,
+    grads, d_rows, back, back_in, tap_send, tap_recv,
     front_sem, in_sem, out_sem, back_sem, tap_sem, lag_sem,
 ):
     me = lax.axis_index("ctx")
@@ -74,8 +92,24 @@
             barrier, inc=1, device_id=(me, lax.rem(rep + k, REPS)), device_id_type=MESH
         )
 
-    def arrange(step, packed):
-        packed = list(packed)
+    row, col = ids(LANES, LANES)
+    m_early[0:LANES, 0:LANES] = ones_where(col == row + 1)
+    m_early[0:LANES, LANES:] = ones_where(col == row + 2)
+    m_early[LANES:, 0:LANES] = ones_where((col == 0) & (row % 2 == 1))
+    m_early[LANES:, LANES:] = ones_where((col < 2) & (col == row % 2))
+    for k in range(2):
+        rows = slice(k * LANES, (k + 1) * LANES)
+        m_late[rows, 0:LANES] = ones_where(col == row - 1)
+        m_late[rows, LANES:] = ones_where(col == row - 2)
+        m_next[rows, 0:LANES] = ones_where((col == LANES - 1) & (row % 2 == 0))
+        m_next[rows, LANES:] = ones_where((col >= LANES - 2) & (col % 2 == row % 2))
+        m_first[rows, :] = ones_where(row == col % 2)
+    last = ones_where(row - (LANES - 2) == col % 2)
+    for k in range(9):
+        m_col[:, k * LANES : (k + 1) * LANES] = ones_where((row < 27) & (row % 9 == k))
+        m_sum[2 * k * LANES : 2 * (k + 1) * LANES, :] = ones_where(ids(256, LANES)[1] == k)
+
+    def arrange(step, _):
         for half in range(4):
             pair = step * 4 + half
             rows = pl.ds(pl.multiple_of(pair * 16, 16), 16)
@@ -85,27 +119,51 @@
                     block = feat[j, g, rows, :] if j < 3 else cot[g, rows, :]
                     wide.append(block.astype(F32))
                 for u in range(2):
-                    shard = pair * 2 + u
-                    for gp in range(2):
-                        tiles = swap_halves(
+                    both = [
+                        swap_halves(
                             wide[2 * gp][8 * u : 8 * u + 8], wide[2 * gp + 1][8 * u : 8 * u + 8]
                         )
-                        for c in range(CHUNKS):
-                            sig[j, c, shard, 8 * gp : 8 * gp + 8, :] = tiles[c]
-                            if j < 3:
-                                at = (c * 3 + j) * 2 + gp
-                                moved = pltpu.roll(tiles[c], lax.rem(2 * shard + 2, LANES), 1)
-                                packed[at] = jnp.where(lane // 2 == shard, moved, packed[at])
-        return tuple(packed)
+                        for gp in range(2)
+                    ]
+                    for c in range(CHUNKS):
+                        sig[j, c, pair * 2 + u] = jnp.concatenate(
+                            [both[0][c], both[1][c]], axis=0
+                        ).astype(BF16)
+        return 0
 
     zero = jnp.zeros((8, LANES), F32)
-    packed = lax.fori_loop(0, SHARDS // 8, arrange, (zero,) * 12)
-    for at in range(12):
-        front[8 * at : 8 * at + 8, :] = packed[at]
+    lax.fori_loop(0, SHARDS // 8, arrange, 0)
+
+    def eight(ref, *at):
+        return ref[at].reshape(8 * 16, LANES)
+
+    def own_lanes(step):
+        rows, cols = ids(8 * 16, LANES)
+        return cols // 2 == step * 8 + rows // 16
+
+    def gather(values):
+        total = values[0:16]
+        for u in range(1, 8):
+            total = total + values[16 * u : 16 * u + 16]
+        return total
+
+    def pack_front(step, _):
+        mine = own_lanes(step)
+        shards = pl.ds(pl.multiple_of(step * 8, 8), 8)
+        for c in range(CHUNKS):
+            for j in range(3):
+                spread_out = product_of(eight(sig, j, c, shards), last)
+                halo[c * 3 + j] += gather(jnp.where(mine, spread_out, 0.0))
+        return 0
+
+    halo[...] = jnp.zeros(halo.shape, F32)
+    lax.fori_loop(0, SHARDS // 8, pack_front, 0)
+    for at in range(6):
+        front[at] = halo[at].astype(BF16)
 
     @pl.when(me == 0)
     def _():
-        front_in[...] = jnp.zeros(front_in.shape, F32)
+        front_in[...] = jnp.zeros(front_in.shape, BF16)
 
     @pl.when(me == SHARDS - 1)
     def _():
@@ -133,12 +191,23 @@
         for u in range(8):
             shard = step * 8 + u
             tile = tcol[pl.ds(pl.multiple_of(shard * 8, 8), 8), :]
+            made = ([], [])
             for gp in range(2):
                 first = tile if gp == 0 else pltpu.roll(tile, LANES - 18 * gp, 1)
                 second = pltpu.roll(tile, LANES - 18 * gp - 9, 1)
-                both = swap_halves(first, second)
-                for c in range(CHUNKS):
-                    wts[c, shard, 8 * gp : 8 * gp + 8, :] = both[c]
+                for c, weight in enumerate(swap_halves(first, second)):
+                    high_part = weight.astype(BF16).astype(F32)
+                    rest = weight - high_part
+                    mid_part = rest.astype(BF16).astype(F32)
+                    rest = rest - mid_part
+                    three = jnp.where(
+                        lane < 9,
+                        high_part,
+                        jnp.where(lane < 18, pltpu.roll(mid_part, 9, 1), pltpu.roll(rest, 18, 1)),
+                    )
+                    made[c].append(jnp.where(lane < 27, three, 0.0))
+            for c in range(CHUNKS):
+                wts[c, shard] = jnp.concatenate(made[c], axis=0).astype(BF16)
         return 0
 
     lax.fori_loop(0, SHARDS // 8, arrange_taps, 0)
@@ -183,33 +252,29 @@
         dst[c, me] = src[c, me]
 
     def short_conv(c, step, _):
+        group = lax.rem(me // GROUP + step, SHARDS // GROUP)
+        shards = pl.ds(pl.multiple_of(group * GROUP, GROUP), GROUP)
+        mine = own_lanes(group)
+        weight = product_of(eight(wts, c, shards), m_col[...])
+        mix = []
+        for j in range(3):
+            here = eight(sig, j, c, shards)
+            before = jnp.concatenate([front_in[c * 3 + j].astype(F32)] * 8, axis=0)
+            before = jnp.where(mine, before, 0.0).astype(BF16)
+            moved = product_of(jnp.concatenate([here, before], axis=1), m_early[...])
+            three = [weight[:, (3 * j + i) * LANES : (3 * j + i + 1) * LANES] for i in range(3)]
+            mix.append(
+                three[0] * here.astype(F32)
+                + three[1] * moved[:, 0:LANES]
+                + three[2] * moved[:, LANES:]
+            )
+        mixed[0, c, shards] = mix[1].reshape(8, 16, LANES)
+        mixed[1, c, shards] = mix[2].reshape(8, 16, LANES)
+        send_in[c, shards, 0:16, :] = (mix[1] * mix[2]).astype(BF16).reshape(8, 16, LANES)
+        gated = eight(sig, 3, c, shards).astype(F32) * mix[0]
+        send_in[c, shards, 16:32, :] = gated.astype(BF16).reshape(8, 16, LANES)
         for u in range(GROUP):
-            shard = lax.rem(me + step * GROUP + u, SHARDS)
-            made = []
-            for gp in range(2):
-                rows = slice(8 * gp, 8 * gp + 8)
-                weight = wts[c, shard, rows, :]
-                mix = []
-                for j in range(3):
-                    here = sig[j, c, shard, rows, :]
-                    at = (c * 3 + j) * 2 + gp
-                    before = pltpu.roll(front_in[8 * at : 8 * at + 8, :], 126 - 2 * shard, 1)
-                    one = pltpu.roll(jnp.where(lane == 127, before, here), 1, 1)
-                    two = pltpu.roll(jnp.where(lane >= 126, before, here), 2, 1)
-                    mix.append(
-                        column(weight, 3 * j) * here
-                        + column(weight, 3 * j + 1) * one
-                        + column(weight, 3 * j + 2) * two
-                    )
-                mixed[0, c, shard, rows, :] = mix[1]
-                mixed[1, c, shard, rows, :] = mix[2]
-                made.append((mix[1] * mix[2], sig[3, c, shard, rows, :] * mix[0]))
-            for a in range(2):
-                send_in[c, shard, 16 * a : 16 * a + 16, :] = jnp.concatenate(
-                    [made[0][a], made[1][a]], axis=0
-                ).astype(BF16)
-        for u in range(GROUP):
-            shard = lax.rem(me + step * GROUP + u, SHARDS)
+            shard = group * GROUP + lax.rem(me + u, GROUP)
 
             @pl.when(shard != me)
             def _():
@@ -429,25 +494,20 @@
         lag_copy(lax.rem(rep + k, REPS)).start()
     lag_recv[rep] = lag_send[rep]
 
-    def make_grads(c, step, packed):
-        packed = list(packed)
-        for u in range(GROUP):
-            shard = step * GROUP + u
-            conv_rows = recv_out[c, shard, 0:16, :].astype(F32)
-            grad_rows = recv_out[c, shard, 16:32, :].astype(F32)
-            for gp in range(2):
-                rows = slice(8 * gp, 8 * gp + 8)
-                value = grad_rows[rows]
-                three = (
-                    sig[3, c, shard, rows, :] * conv_rows[rows],
-                    value * mixed[1, c, shard, rows, :],
-                    value * mixed[0, c, shard, rows, :],
-                )
-                for j in range(3):
-                    grads[c, j, shard, rows, :] = three[j]
-                    moved = pltpu.roll(three[j], 2 * shard, 1)
-                    packed[2 * j + gp] = jnp.where(lane // 2 == shard, moved, packed[2 * j + gp])
-        return tuple(packed)
+    def make_grads(c, step, _):
+        shards = pl.ds(pl.multiple_of(step * 8, 8), 8)
+        mine = own_lanes(step)
+        value = recv_out[c, shards, 16:32, :].astype(F32)
+        three = (
+            sig[3, c, shards].astype(F32) * recv_out[c, shards, 0:16, :].astype(F32),
+            value * mixed[1, c, shards],
+            value * mixed[0, c, shards],
+        )
+        for j in range(3):
+            grads[c, j, shards] = three[j]
+            spread_out = product_of(halves(three[j].reshape(8 * 16, LANES)), m_first[...])
+            back[c, j] += gather(jnp.where(mine, spread_out, 0.0))
+        return 0
 
     def back_copy(c):
         return pltpu.make_async_remote_copy(
@@ -458,41 +518,40 @@
 
     def post_first(c):
         all_copies(send_out, recv_out, out_sem, c).wait_recv()
-        packed = lax.fori_loop(
-            0, SHARDS // GROUP, functools.partial(make_grads, c), (zero,) * 6
-        )
-        for at in range(6):
-            back[c, 8 * at : 8 * at + 8, :] = packed[at]
+        back[c] = jnp.zeros(back.shape[1:], F32)
+        lax.fori_loop(0, SHARDS // GROUP, functools.partial(make_grads, c), 0)
 
         @pl.when(me > 0)
         def _():
             back_copy(c).start()
 
     def short_back(c, step, _):
-        for u in range(GROUP):
-            shard = step * GROUP + u
-            sums = tap_send[shard] if c == 1 else zero
-            for gp in range(2):
-                rows = slice(8 * gp, 8 * gp + 8)
-                weight = wts[c, shard, rows, :]
-                for j in range(3):
-                    here = grads[c, j, shard, rows, :]
-                    at = 2 * j + gp
-                    after = pltpu.roll(
-                        back_in[c, 8 * at : 8 * at + 8, :], lax.rem(LANES - 2 * shard, LANES), 1
-                    )
-                    one = pltpu.roll(jnp.where(lane == 0, after, here), LANES - 1, 1)
-                    two = pltpu.roll(jnp.where(lane < 2, after, here), LANES - 2, 1)
-                    grads[c, j, shard, rows, :] = (
-                        column(weight, 3 * j) * here
-                        + column(weight, 3 * j + 1) * one
-                        + column(weight, 3 * j + 2) * two
-                    )
-                    signal = sig[j, c, shard, rows, :]
-                    for i, moved in enumerate((here, one, two)):
-                        share = jnp.sum(moved * signal, axis=1, keepdims=True)
-                        sums = jnp.where(lane == c * 18 + gp * 9 + 3 * j + i, share, sums)
-            tap_send[shard] = sums
+        shards = pl.ds(pl.multiple_of(step * 8, 8), 8)
+        mine = own_lanes(step)
+        weight = product_of(eight(wts, c, shards), m_col[...])
+        sums = jnp.zeros((8 * 16, LANES), F32)
+        for j in range(3):
+            here = eight(grads, c, j, shards)
+            after = jnp.where(mine, jnp.concatenate([back_in[c, j]] * 8, axis=0), 0.0)
+            moved = product_of(halves(here), m_late[...]) + product_of(halves(after), m_next[...])
+            three = (here, moved[:, 0:LANES], moved[:, LANES:])
+            signal = eight(sig, j, c, shards).astype(F32)
+            total = None
+            for i in range(3):
+                k = 3 * j + i
+                term = weight[:, k * LANES : (k + 1) * LANES] * three[i]
+                total = term if i == 0 else total + term
+                sums = sums + product_of(
+                    halves(three[i] * signal), m_sum[2 * k * LANES : 2 * (k + 1) * LANES, :]
+                )
+            d_rows[c, j, shards] = total.astype(BF16).reshape(8, 16, LANES)
+        for u in range(8):
+            first = sums[16 * u : 16 * u + 8]
+            second = pltpu.roll(sums[16 * u + 8 : 16 * u + 16], 18 * c + 9, 1)
+            if c == 0:
+                tap_send[step * 8 + u] = first + second
+            else:
+                tap_send[step * 8 + u] += pltpu.roll(first, 18 * c, 1) + second
         return 0
 
     def post_second(c):
@@ -525,11 +584,14 @@
             pair = step * 4 + half
             rows = pl.ds(pl.multiple_of(pair * 16, 16), 16)
             for j in range(3):
+                chunk = [
+                    [d_rows[c, j, pair * 2 + u].astype(F32) for u in range(2)]
+                    for c in range(CHUNKS)
+                ]
                 for gp in range(2):
                     tiles = [
                         swap_halves(
-                            grads[0, j, pair * 2 + u, 8 * gp : 8 * gp + 8, :],
-                            grads[1, j, pair * 2 + u, 8 * gp : 8 * gp + 8, :],
+                            chunk[0][u][8 * gp : 8 * gp + 8], chunk[1][u][8 * gp : 8 * gp + 8]
                         )
                         for u in range(2)
                     ]
@@ -591,14 +653,21 @@
         in_specs=[vmem, vmem, vmem, pl.BlockSpec(memory_space=pltpu.SMEM), vmem],
         out_specs=(vmem,) * 4,
         scratch_shapes=[
-            pltpu.VMEM((4, CHUNKS, SHARDS, 16, LANES), F32),
+            pltpu.VMEM((4, CHUNKS, SHARDS, 16, LANES), BF16),
             pltpu.VMEM((2, CHUNKS, SHARDS, 16, LANES), F32),
-            pltpu.VMEM((CHUNKS, SHARDS, 16, LANES), F32),
+            pltpu.VMEM((CHUNKS, SHARDS, 16, LANES), BF16),
             pltpu.VMEM((512, LANES), F32),
             pltpu.VMEM((8, LANES, LANES + 8192), BF16),
             pltpu.VMEM((8, LANES + 8192), F32),
-            pltpu.VMEM((96, LANES), F32),
-            pltpu.VMEM((96, LANES), F32),
+            pltpu.VMEM((6, 16, LANES), BF16),
+            pltpu.VMEM((6, 16, LANES), BF16),
+            pltpu.VMEM((6, 16, LANES), F32),
+            pltpu.VMEM((256, 256), BF16),
+            pltpu.VMEM((LANES, 9 * LANES), BF16),
+            pltpu.VMEM((256, 256), BF16),
+            pltpu.VMEM((256, 256), BF16),
+            pltpu.VMEM((256, LANES), BF16),
+            pltpu.VMEM((18 * LANES, LANES), BF16),
             message, message, message, message,
             pltpu.VMEM((2, 1024, LANES), F32),
             pltpu.VMEM((2, 512, LANES), F32),
@@ -615,8 +684,9 @@
             pltpu.VMEM((REPS, 8, 16, LANES), BF16),
             pltpu.VMEM((REPS, 8, 16, LANES), BF16),
             pltpu.VMEM((CHUNKS, 3, SHARDS, 16, LANES), F32),
-            pltpu.VMEM((CHUNKS, 48, LANES), F32),
-            pltpu.VMEM((CHUNKS, 48, LANES), F32),
+            pltpu.VMEM((CHUNKS, 3, SHARDS, 16, LANES), BF16),
+            pltpu.VMEM((CHUNKS, 3, 16, LANES), F32),
+            pltpu.VMEM((CHUNKS, 3, 16, LANES), F32),
             pltpu.VMEM((SHARDS, 8, LANES), F32),
             pltpu.VMEM((SHARDS, 8, LANES), F32),
             pltpu.SemaphoreType.DMA((2,)),

time: 190 us -> 110 us (0.58); the launches traced: 190 us -> 108 us
  Pallas kernels: 180 us -> 98.3 us
    pallas_call x1, Pallas kernels: 180 us -> 98.3 us  [per_device(): pl.pallas_call(kernel, out_shape=(jax.ShapeDtypeStruct((3, 4, 512, LANES)...]
where the time goes in v2:
time: 110 us; the launch traced here: 108 us
  Pallas kernels  98.3 us (89%)
  local copies, waits for them, and re-layouts  8.93 us (8%)
    pallas_call x1, Pallas kernels, per_device(): pl.pallas_call(kernel, out_shape=(jax.ShapeDtypeStruct((3, 4, 512, LANES)...  98.3 us
    unnamed x2, local copies, waits for them, and re-layouts  4.14 us

profile of v2, /device:TPU:1, one launch (start us, length us, event | category | flops | bytes accessed | tf_op | source)
XLA Modules:
  0.0 107.9 jit_solution(14561769202464814771)
XLA Ops:
  0.6 0.9 copy.15
  1.6 0.6 pad.4.taps
  2.3 98.3 %shard_map.84 = (bf16[3,4,512,128]{3,2,1,0:T(8,128)(2,1)}, f32[8,128]{1,0:T(8,128)}, f32[32,128]{1,0:T(8,128)}, f32[8,16,128]{2,1,0:T(8,128)}) custom-call(bf16[3,4,512,128]{3,2,1,0:T(8,128)(2,1)} %feat.1, bf16[4,512,128]{2,1,0:T(8,128)(2,1)} %cot.1, f32[40,512]{1,0:T(8,128)} %pad.4.taps, f32[4,8]{1,0:T(4,128)} %skip.1, f32[8,8192]{1,0:T(8,128)} %filt.1), custom_call_target="tpu_custom_call" | custom-call | tf_op jit(solution)/shard_map/pallas_call | solution.py:645
  100.6 0.8 slice_reduce_fusion
  101.4 0.1 reshape_squeeze.3
  101.5 0.7 reshape.26
  102.2 0.8 copy.16
  103.0 0.1 reshape.24
  103.1 0.7 reshape.25
  103.8 1.5 %copy.21 = f32[1,8,16,128]{3,1,2,0:T(8,128)} copy(f32[1,8,16,128]{3,2,1,0:T(8,128)} %bitcast.14) | data formatting | bytes 131072
  105.3 2.7 %copy.23 = bf16[3,4,512,128]{3,2,1,0:T(8,128)(2,1)} copy(bf16[3,4,512,128]{3,2,1,0:T(8,128)(2,1)} %get-tuple-element.16) | data formatting | bytes 3145728
  (3 shorter events, 0.1 us)

commit v3 on v2

--- a/solution.py
+++ b/solution.py
@@ -18,6 +18,7 @@
 QUAD = 4
 GROUP = 8
 LAGS = 64
+WIDE = 32
 
 
 def lane_ids():
@@ -54,25 +55,20 @@
     return jnp.where(condition, 1.0, 0.0).astype(BF16)
 
 
-def halves(wide):
-    high = wide.astype(BF16)
-    return jnp.concatenate([high, (wide - high.astype(F32)).astype(BF16)], axis=1)
-
-
 def product_of(left, right):
     return jnp.dot(left, right, preferred_element_type=F32)
 
 
 def kernel(
     feat, cot, taps, skip, filt,
-    d_feat, d_short, d_skip, d_filt,
+    d_rows, d_short, d_skip, d_filt,
     sig, mixed, wts, tcol, strip, base, front, front_in, halo,
-    m_early, m_col, m_late, m_next, m_first, m_sum,
+    m_early, m_col, m_late, m_first, m_sum,
     send_in, recv_in, send_out, recv_out,
     spread, prod_nat, grad_nat, xs, conv, merged,
-    shifted, prod_t, cross, low, high, lagrow, lag_send, lag_recv,
-    grads, d_rows, back, back_in, tap_send, tap_recv,
-    front_sem, in_sem, out_sem, back_sem, tap_sem, lag_sem,
+    shifted, prod_t, prod_half, cross, low, high, lagrow, lag_send, lag_recv,
+    grads, early, back, back_out, back_in, taps_all, near_send, near_recv, far_send, far_recv,
+    front_sem, in_sem, out_sem, out_recv_sem, back_sem, near_sem, far_sem, lag_sem,
 ):
     me = lax.axis_index("ctx")
     rep = lax.axis_index("rep")
@@ -93,21 +89,13 @@
         )
 
     row, col = ids(LANES, LANES)
+    last = ones_where(row - (LANES - 2) == col % 2)
     m_early[0:LANES, 0:LANES] = ones_where(col == row + 1)
     m_early[0:LANES, LANES:] = ones_where(col == row + 2)
     m_early[LANES:, 0:LANES] = ones_where((col == 0) & (row % 2 == 1))
     m_early[LANES:, LANES:] = ones_where((col < 2) & (col == row % 2))
-    for k in range(2):
-        rows = slice(k * LANES, (k + 1) * LANES)
-        m_late[rows, 0:LANES] = ones_where(col == row - 1)
-        m_late[rows, LANES:] = ones_where(col == row - 2)
-        m_next[rows, 0:LANES] = ones_where((col == LANES - 1) & (row % 2 == 0))
-        m_next[rows, LANES:] = ones_where((col >= LANES - 2) & (col % 2 == row % 2))
-        m_first[rows, :] = ones_where(row == col % 2)
-    last = ones_where(row - (LANES - 2) == col % 2)
     for k in range(9):
         m_col[:, k * LANES : (k + 1) * LANES] = ones_where((row < 27) & (row % 9 == k))
-        m_sum[2 * k * LANES : 2 * (k + 1) * LANES, :] = ones_where(ids(256, LANES)[1] == k)
 
     def arrange(step, _):
         for half in range(4):
@@ -147,19 +135,22 @@
             total = total + values[16 * u : 16 * u + 16]
         return total
 
-    def pack_front(step, _):
+    def pack_front(c, step, _):
         mine = own_lanes(step)
         shards = pl.ds(pl.multiple_of(step * 8, 8), 8)
-        for c in range(CHUNKS):
-            for j in range(3):
-                spread_out = product_of(eight(sig, j, c, shards), last)
-                halo[c * 3 + j] += gather(jnp.where(mine, spread_out, 0.0))
+        for j in range(3):
+            spread_out = product_of(eight(sig, j, c, shards), last)
+            halo[c, j] += gather(jnp.where(mine, spread_out, 0.0))
         return 0
 
     halo[...] = jnp.zeros(halo.shape, F32)
-    lax.fori_loop(0, SHARDS // 8, pack_front, 0)
-    for at in range(6):
-        front[at] = halo[at].astype(BF16)
+
+    def front_copy(c):
+        return pltpu.make_async_remote_copy(
+            src_ref=front.at[c], dst_ref=front_in.at[c], send_sem=front_sem.at[0, c],
+            recv_sem=front_sem.at[1, c], device_id=(lax.rem(me + 1, SHARDS), rep),
+            device_id_type=MESH,
+        )
 
     @pl.when(me == 0)
     def _():
@@ -167,24 +158,23 @@
 
     @pl.when(me == SHARDS - 1)
     def _():
-        back_in[...] = jnp.zeros(back_in.shape, F32)
-
-    pl.semaphore_wait(barrier, SHARDS - 1 + REPS - 1)
-
-    def front_copy():
-        return pltpu.make_async_remote_copy(
-            src_ref=front, dst_ref=front_in, send_sem=front_sem.at[0], recv_sem=front_sem.at[1],
-            device_id=(lax.rem(me + 1, SHARDS), rep), device_id_type=MESH,
-        )
-
-    @pl.when(me < SHARDS - 1)
-    def _():
-        front_copy().start()
+        back_in[...] = jnp.zeros(back_in.shape, BF16)
+
+    for c in range(CHUNKS):
+        lax.fori_loop(0, SHARDS // 8, functools.partial(pack_front, c), 0)
+        front[c] = halo[c].astype(BF16)
+        if c == 0:
+            pl.semaphore_wait(barrier, SHARDS - 1 + REPS - 1)
+
+        @pl.when(me < SHARDS - 1)
+        def _():
+            front_copy(c).start()
 
     for part in range(4):
         cols = slice(part * LANES, (part + 1) * LANES)
+        rows = [taps[j, i, g : g + 1, cols] for g in range(4) for j in range(3) for i in range(3)]
         tcol[cols, :] = jnp.concatenate(
-            [taps[:, cols], jnp.zeros((LANES - 40, LANES), F32)], axis=0
+            rows + [jnp.zeros((LANES - 36, LANES), F32)], axis=0
         ).T
 
     def arrange_taps(step, _):
@@ -212,44 +202,40 @@
 
     lax.fori_loop(0, SHARDS // 8, arrange_taps, 0)
 
-    for q in range(QUAD):
-        for u in range(2):
-            xs[q, u, 0:256, :] = jnp.zeros((256, 256), BF16)
-        for e in range(2):
-            for k in range(4):
-                shifted[q, e, k, 128:256, :] = jnp.zeros((128, LANES), BF16)
-        high[q, LAGS] = zero
-    for e in range(2):
-        grad_nat[e, 512:576, :] = jnp.zeros((64, LANES), F32)
-
-    @pl.when(me > 0)
-    def _():
-        front_copy().wait_recv()
-
-    @pl.when(me < SHARDS - 1)
-    def _():
-        front_copy().wait_send()
-
-    def block_copy(src, dst, sems, c, peer):
+    def in_copy(c, peer):
         return pltpu.make_async_remote_copy(
-            src_ref=src.at[c, peer], dst_ref=dst.at[c, me], send_sem=sems.at[0, c],
-            recv_sem=sems.at[1, c], device_id=(peer, rep), device_id_type=MESH,
-        )
-
-    def all_copies(src, dst, sems, c):
+            src_ref=send_in.at[c, peer], dst_ref=recv_in.at[c, me], send_sem=in_sem.at[0, c],
+            recv_sem=in_sem.at[1, c], device_id=(peer, rep), device_id_type=MESH,
+        )
+
+    def out_copy(c, peer):
+        return pltpu.make_async_remote_copy(
+            src_ref=send_out.at[c, peer], dst_ref=recv_out.at[c, me], send_sem=out_sem.at[c],
+            recv_sem=out_recv_sem.at[c, me // GROUP], device_id=(peer, rep), device_id_type=MESH,
+        )
+
+    def in_copies(c):
         others = pl.ds(0, SHARDS - 1)
         return pltpu.make_async_remote_copy(
-            src_ref=src.at[c, others], dst_ref=dst.at[c, others], send_sem=sems.at[0, c],
-            recv_sem=sems.at[1, c], device_id=(lax.rem(me + 1, SHARDS), rep), device_id_type=MESH,
-        )
-
-    def send_all(src, dst, sems, c):
+            src_ref=send_in.at[c, others], dst_ref=recv_in.at[c, others], send_sem=in_sem.at[0, c],
+            recv_sem=in_sem.at[1, c], device_id=(lax.rem(me + 1, SHARDS), rep), device_id_type=MESH,
+        )
+
+    def out_copies(c, group, count):
+        some = pl.ds(0, count)
+        return pltpu.make_async_remote_copy(
+            src_ref=send_out.at[c, some], dst_ref=recv_out.at[c, some], send_sem=out_sem.at[c],
+            recv_sem=out_recv_sem.at[c, group], device_id=(lax.rem(me + 1, SHARDS), rep),
+            device_id_type=MESH,
+        )
+
+    def send_results(c):
         def one(k, _):
-            block_copy(src, dst, sems, c, lax.rem(me + k, SHARDS)).start()
+            out_copy(c, lax.rem(me + k, SHARDS)).start()
             return 0
 
         lax.fori_loop(1, SHARDS, one, 0)
-        dst[c, me] = src[c, me]
+        recv_out[c, me] = send_out[c, me]
 
     def short_conv(c, step, _):
         group = lax.rem(me // GROUP + step, SHARDS // GROUP)
@@ -259,9 +245,13 @@
         mix = []
         for j in range(3):
             here = eight(sig, j, c, shards)
-            before = jnp.concatenate([front_in[c * 3 + j].astype(F32)] * 8, axis=0)
+            before = jnp.concatenate([front_in[c, j].astype(F32)] * 8, axis=0)
             before = jnp.where(mine, before, 0.0).astype(BF16)
             moved = product_of(jnp.concatenate([here, before], axis=1), m_early[...])
+            for i in range(2):
+                early[c, j, i, shards] = (
+                    moved[:, i * LANES : (i + 1) * LANES].astype(BF16).reshape(8, 16, LANES)
+                )
             three = [weight[:, (3 * j + i) * LANES : (3 * j + i + 1) * LANES] for i in range(3)]
             mix.append(
                 three[0] * here.astype(F32)
@@ -278,11 +268,16 @@
 
             @pl.when(shard != me)
             def _():
-                block_copy(send_in, recv_in, in_sem, c, shard).start()
+                in_copy(c, shard).start()
 
         return 0
 
     for c in range(CHUNKS):
+
+        @pl.when(me > 0)
+        def _():
+            front_copy(c).wait_recv()
+
         lax.fori_loop(0, SHARDS // GROUP, functools.partial(short_conv, c), 0)
         recv_in[c, me] = send_in[c, me]
 
@@ -311,17 +306,33 @@
 
     lax.fori_loop(0, 8, make_strip, 0)
 
+    m_late[0:LANES, 0:LANES] = ones_where(col == row - 1)
+    m_late[0:LANES, LANES:] = ones_where(col == row - 2)
+    m_late[LANES:, 0:LANES] = ones_where((col == LANES - 1) & (row % 2 == 0))
+    m_late[LANES:, LANES:] = ones_where((col >= LANES - 2) & (col % 2 == row % 2))
+    m_first[...] = ones_where(row == col % 2)
+    for k in range(9):
+        m_sum[k * LANES : (k + 1) * LANES, :] = ones_where(col == k)
+
+    for q in range(QUAD):
+        for u in range(2):
+            xs[q, u, 0:256, :] = jnp.zeros((256, 256), BF16)
+        for e in range(2):
+            for k in range(4):
+                shifted[q, e, k, 128:256, :] = jnp.zeros((128, LANES), BF16)
+        high[q, LAGS] = zero
+    for e in range(2):
+        grad_nat[e, 512:576, :] = jnp.zeros((64, LANES), F32)
+
     flip = flip_matrix()
     sign_row = lax.broadcasted_iota(jnp.int32, (8, 256), 0) % 4
 
     def unpack(c, step, total):
-        back_rows = jnp.concatenate(
-            [recv_in[c, step * 8 + u, 16:32, :] for u in range(8)], axis=0
-        )
-        turned = jnp.dot(back_rows, flip, preferred_element_type=F32)
-        for u in range(8):
-            shard = step * 8 + u
-            place = step * 4 + u // 2
+        first = pl.ds(pl.multiple_of(step * WIDE, WIDE), WIDE)
+        turned = product_of(recv_in[c, first, 16:32, :].reshape(WIDE * 16, LANES), flip)
+        for u in range(WIDE):
+            shard = step * WIDE + u
+            place = step * (WIDE // 2) + u // 2
             e = u % 2
             product = recv_in[c, shard, 0:16, :].astype(F32)
             gated = recv_in[c, shard, 16:32, :].astype(F32)
@@ -363,26 +374,22 @@
         return 0
 
     def pack(c, step, _):
-        turned = jnp.concatenate(
-            [
-                merged[u % 2, pl.ds(pl.multiple_of((step * 4 + u // 2) * 32 + 16, 16), 16), :]
-                for u in range(8)
-            ],
-            axis=0,
+        half = WIDE // 2
+        rows = pl.ds(pl.multiple_of(step * half * 32, 32), half * 32)
+        both = [merged[e, rows, :].astype(BF16).reshape(half, 32, LANES) for e in range(2)]
+        turned = product_of(
+            jnp.concatenate([b[:, 16:32].reshape(half * 16, LANES) for b in both], axis=0), flip
         ).astype(BF16)
-        turned = jnp.dot(turned, flip, preferred_element_type=F32).astype(BF16)
-        for u in range(8):
-            shard = step * 8 + u
-            place = step * 4 + u // 2
-            send_out[c, shard, 0:16, :] = merged[
-                u % 2, pl.ds(pl.multiple_of(place * 32, 32), 16), :
-            ].astype(BF16)
-            send_out[c, SHARDS - 1 - shard, 16:32, :] = turned[16 * u : 16 * u + 16]
+        for u in range(WIDE):
+            shard = step * WIDE + u
+            at = (u % 2) * half + u // 2
+            send_out[c, shard, 0:16, :] = both[u % 2][u // 2, 0:16]
+            send_out[c, SHARDS - 1 - shard, 16:32, :] = turned[16 * at : 16 * at + 16]
         return 0
 
     def owner_conv(c):
-        all_copies(send_in, recv_in, in_sem, c).wait_recv()
-        total = lax.fori_loop(0, 8, functools.partial(unpack, c), jnp.zeros((16, LANES), F32))
+        in_copies(c).wait_recv()
+        total = lax.fori_loop(0, SHARDS // WIDE, functools.partial(unpack, c), jnp.zeros((16, LANES), F32))
         d_skip[16 * c : 16 * c + 16, :] = jnp.broadcast_to(
             jnp.sum(total, axis=1, keepdims=True), (16, LANES)
         )
@@ -398,24 +405,22 @@
         for q in range(QUAD):
             for e in range(2):
                 merged[e, pl.ds(q, 256, stride=4), :] = conv[q, :, LANES * e : LANES * e + LANES]
-        lax.fori_loop(0, 8, functools.partial(pack, c), 0)
-        send_all(send_out, recv_out, out_sem, c)
+        lax.fori_loop(0, SHARDS // WIDE, functools.partial(pack, c), 0)
+        send_results(c)
 
     def cross_dots(q, m, slot):
+        rows = 128 if m < 4 else 64
+        left = prod_t if m < 4 else prod_half
         for pair in range(4):
             sides = []
             for odd in range(2):
-                lag = 2 * pair + odd
-                half = pair
                 parts = []
                 for e in range(2):
-                    carry = half + (1 if e == 1 and odd == 1 else 0)
-                    at = pl.multiple_of(16 * m + 16 * (carry // 4), 16)
-                    parts.append(shifted[q, (e + odd) % 2, carry % 4, pl.ds(at, 128), :])
+                    carry = pair + (1 if e == 1 and odd == 1 else 0)
+                    at = 16 * m + 16 * (carry // 4)
+                    parts.append(shifted[q, (e + odd) % 2, carry % 4, at : at + rows, :])
                 sides.append(jnp.concatenate(parts, axis=0))
-            cross[slot, pair] = jnp.dot(
-                prod_t[q], jnp.concatenate(sides, axis=1), preferred_element_type=F32
-            )
+            cross[slot, pair] = product_of(left[q], jnp.concatenate(sides, axis=1))
 
     def diagonals(q, m, slot):
         for lag in range(8):
@@ -435,23 +440,25 @@
                 prod_t[q, :, LANES * e : LANES * e + LANES] = (
                     prod_nat[e, pl.ds(q, 128, stride=4), :].T.astype(BF16)
                 )
+                prod_half[q, :, 64 * e : 64 * e + 64] = (
+                    prod_nat[e, pl.ds(q, 64, stride=4), :].T.astype(BF16)
+                )
                 for k in range(4):
                     shifted[q, e, k, 0:128, :] = grad_nat[
                         e, pl.ds(q + 16 * k, 128, stride=4), :
                     ].astype(BF16)
         cross_dots(0, 0, 0)
 
-        def two(step, _):
-            q = step // 4
-            m = 2 * (step % 4)
-            cross_dots(q, m + 1, 1)
-            diagonals(q, m, 0)
-            later = jnp.minimum(step + 1, 15)
-            cross_dots(later // 4, 2 * (later % 4), 0)
-            diagonals(q, m + 1, 1)
+        def one_filter(q, _):
+            for m in range(8):
+                if m < 7:
+                    cross_dots(q, m + 1, (m + 1) % 2)
+                else:
+                    cross_dots(jnp.minimum(q + 1, QUAD - 1), 0, 0)
+                diagonals(q, m, m % 2)
             return 0
 
-        lax.fori_loop(0, 16, two, 0)
+        lax.fori_loop(0, QUAD, one_filter, 0)
 
         def turn(step, _):
             q = step // 4
@@ -495,31 +502,56 @@
     lag_recv[rep] = lag_send[rep]
 
     def make_grads(c, step, _):
-        shards = pl.ds(pl.multiple_of(step * 8, 8), 8)
-        mine = own_lanes(step)
+        own = me // GROUP
+        group = lax.rem(own + GROUP - 1 - step, GROUP)
+
+        @pl.when(group == own)
+        def _():
+            out_copies(c, group, GROUP - 1).wait_recv()
+
+        @pl.when(group != own)
+        def _():
+            out_copies(c, group, GROUP).wait_recv()
+
+        shards = pl.ds(pl.multiple_of(group * 8, 8), 8)
+        mine = own_lanes(group)
         value = recv_out[c, shards, 16:32, :].astype(F32)
         three = (
             sig[3, c, shards].astype(F32) * recv_out[c, shards, 0:16, :].astype(F32),
             value * mixed[1, c, shards],
             value * mixed[0, c, shards],
         )
+        terms = []
         for j in range(3):
-            grads[c, j, shards] = three[j]
-            spread_out = product_of(halves(three[j].reshape(8 * 16, LANES)), m_first[...])
+            narrow = three[j].astype(BF16)
+            grads[c, j, shards] = narrow
+            spread_out = product_of(narrow.reshape(8 * 16, LANES), m_first[...])
             back[c, j] += gather(jnp.where(mine, spread_out, 0.0))
+            wide = three[j].reshape(8 * 16, LANES)
+            terms.append((wide * eight(sig, j, c, shards).astype(F32)).astype(BF16))
+            for i in range(2):
+                terms.append((wide * eight(early, c, j, i, shards).astype(F32)).astype(BF16))
+        sums = product_of(jnp.concatenate(terms, axis=1), m_sum[...])
+        for u in range(8):
+            first = sums[16 * u : 16 * u + 8]
+            second = pltpu.roll(sums[16 * u + 8 : 16 * u + 16], 18 * c + 9, 1)
+            if c == 0:
+                taps_all[group * 8 + u] = first + second
+            else:
+                taps_all[group * 8 + u] += pltpu.roll(first, 18 * c, 1) + second
         return 0
 
     def back_copy(c):
         return pltpu.make_async_remote_copy(
-            src_ref=back.at[c], dst_ref=back_in.at[c], send_sem=back_sem.at[0, c],
+            src_ref=back_out.at[c], dst_ref=back_in.at[c], send_sem=back_sem.at[0, c],
             recv_sem=back_sem.at[1, c],
             device_id=(lax.rem(me + SHARDS - 1, SHARDS), rep), device_id_type=MESH,
         )
 
-    def post_first(c):
-        all_copies(send_out, recv_out, out_sem, c).wait_recv()
+    def grads_of(c):
         back[c] = jnp.zeros(back.shape[1:], F32)
         lax.fori_loop(0, SHARDS // GROUP, functools.partial(make_grads, c), 0)
+        back_out[c] = back[c].astype(BF16)
 
         @pl.when(me > 0)
         def _():
@@ -529,79 +561,79 @@
         shards = pl.ds(pl.multiple_of(step * 8, 8), 8)
         mine = own_lanes(step)
         weight = product_of(eight(wts, c, shards), m_col[...])
-        sums = jnp.zeros((8 * 16, LANES), F32)
         for j in range(3):
             here = eight(grads, c, j, shards)
-            after = jnp.where(mine, jnp.concatenate([back_in[c, j]] * 8, axis=0), 0.0)
-            moved = product_of(halves(here), m_late[...]) + product_of(halves(after), m_next[...])
-            three = (here, moved[:, 0:LANES], moved[:, LANES:])
-            signal = eight(sig, j, c, shards).astype(F32)
-            total = None
-            for i in range(3):
-                k = 3 * j + i
-                term = weight[:, k * LANES : (k + 1) * LANES] * three[i]
-                total = term if i == 0 else total + term
-                sums = sums + product_of(
-                    halves(three[i] * signal), m_sum[2 * k * LANES : 2 * (k + 1) * LANES, :]
-                )
+            after = jnp.concatenate([back_in[c, j].astype(F32)] * 8, axis=0)
+            after = jnp.where(mine, after, 0.0).astype(BF16)
+            moved = product_of(jnp.concatenate([here, after], axis=1), m_late[...])
+            at = 3 * j * LANES
+            total = (
+                weight[:, at : at + LANES] * here.astype(F32)
+                + weight[:, at + LANES : at + 2 * LANES] * moved[:, 0:LANES]
+                + weight[:, at + 2 * LANES : at + 3 * LANES] * moved[:, LANES:]
+            )
             d_rows[c, j, shards] = total.astype(BF16).reshape(8, 16, LANES)
-        for u in range(8):
-            first = sums[16 * u : 16 * u + 8]
-            second = pltpu.roll(sums[16 * u + 8 : 16 * u + 16], 18 * c + 9, 1)
-            if c == 0:
-                tap_send[step * 8 + u] = first + second
-            else:
-                tap_send[step * 8 + u] += pltpu.roll(first, 18 * c, 1) + second
-        return 0
-
-    def post_second(c):
+        return 0
+
+    def features_of(c):
         @pl.when(me < SHARDS - 1)
         def _():
             back_copy(c).wait_recv()
 
         lax.fori_loop(0, SHARDS // GROUP, functools.partial(short_back, c), 0)
 
-    post_first(0)
-    post_first(1)
-    post_second(0)
-    post_second(1)
-
-    def tap_copy(peer):
+    grads_of(0)
+    features_of(0)
+    grads_of(1)
+
+    own_group = me // GROUP
+    own_place = lax.rem(me, GROUP)
+
+    def near_copy(place):
         return pltpu.make_async_remote_copy(
-            src_ref=tap_send.at[peer], dst_ref=tap_recv.at[me], send_sem=tap_sem.at[0],
-            recv_sem=tap_sem.at[1], device_id=(peer, rep), device_id_type=MESH,
-        )
-
-    def send_taps(k, _):
-        tap_copy(lax.rem(me + k, SHARDS)).start()
-        return 0
-
-    lax.fori_loop(1, SHARDS, send_taps, 0)
-    tap_recv[me] = tap_send[me]
-
-    def put_back(step, _):
-        for half in range(4):
-            pair = step * 4 + half
-            rows = pl.ds(pl.multiple_of(pair * 16, 16), 16)
-            for j in range(3):
-                chunk = [
-                    [d_rows[c, j, pair * 2 + u].astype(F32) for u in range(2)]
-                    for c in range(CHUNKS)
-                ]
-                for gp in range(2):
-                    tiles = [
-                        swap_halves(
-                            chunk[0][u][8 * gp : 8 * gp + 8], chunk[1][u][8 * gp : 8 * gp + 8]
-                        )
-                        for u in range(2)
-                    ]
-                    for g in range(2):
-                        d_feat[j, 2 * gp + g, rows, :] = jnp.concatenate(
-                            [tiles[0][g], tiles[1][g]], axis=0
-                        ).astype(BF16)
-        return 0
-
-    lax.fori_loop(0, SHARDS // 8, put_back, 0)
+            src_ref=near_send.at[place], dst_ref=near_recv.at[own_place], send_sem=near_sem.at[0],
+            recv_sem=near_sem.at[1], device_id=(own_group * GROUP + place, rep),
+            device_id_type=MESH,
+        )
+
+    def far_copy(group):
+        return pltpu.make_async_remote_copy(
+            src_ref=far_send.at[group], dst_ref=far_recv.at[own_group], send_sem=far_sem.at[0],
+            recv_sem=far_sem.at[1], device_id=(group * GROUP + own_place, rep),
+            device_id_type=MESH,
+        )
+
+    for place in range(GROUP):
+        for m in range(3):
+            tile = taps_all[3 * m * GROUP + place]
+            for n in range(1, 3 if m < 2 else 2):
+                tile = tile + pltpu.roll(taps_all[(3 * m + n) * GROUP + place], 36 * n, 1)
+            near_send[place, 8 * m : 8 * m + 8, :] = tile
+    for k in range(1, GROUP):
+        near_copy(lax.rem(own_place + k, GROUP)).start()
+    near_recv[own_place] = near_send[own_place]
+
+    features_of(1)
+
+    seven = pl.ds(0, GROUP - 1)
+    near_all = pltpu.make_async_remote_copy(
+        src_ref=near_send.at[seven], dst_ref=near_recv.at[seven], send_sem=near_sem.at[0],
+        recv_sem=near_sem.at[1], device_id=(lax.rem(me + 1, SHARDS), rep), device_id_type=MESH,
+    )
+    far_all = pltpu.make_async_remote_copy(
+        src_ref=far_send.at[seven], dst_ref=far_recv.at[seven], send_sem=far_sem.at[0],
+        recv_sem=far_sem.at[1], device_id=(lax.rem(me + 1, SHARDS), rep), device_id_type=MESH,
+    )
+    near_all.wait_recv()
+    packed = jnp.sum(near_recv[...], axis=0)
+    for group in range(GROUP):
+        tile = packed[8 * (group // 3) : 8 * (group // 3) + 8]
+        if group % 3:
+            tile = pltpu.roll(tile, LANES - 36 * (group % 3), 1)
+        far_send[group] = jnp.where(lane < 36, tile, 0.0)
+    for k in range(1, GROUP):
+        far_copy(lax.rem(own_group + k, GROUP)).start()
+    far_recv[own_group] = far_send[own_group]
 
     lag_all = pltpu.make_async_remote_copy(
         src_ref=lag_send.at[pl.ds(0, REPS - 1)], dst_ref=lag_recv.at[pl.ds(0, REPS - 1)],
@@ -610,45 +642,86 @@
     )
     lag_all.wait_recv()
     for f in range(8):
-        d_filt[f] = (
+        d_filt[16 * f : 16 * f + 16, :] = (
             lag_recv[0, f].astype(F32)
             + lag_recv[1, f].astype(F32)
             + lag_recv[2, f].astype(F32)
             + lag_recv[3, f].astype(F32)
         )
 
-    tap_all = pltpu.make_async_remote_copy(
-        src_ref=tap_send.at[pl.ds(0, SHARDS - 1)], dst_ref=tap_recv.at[pl.ds(0, SHARDS - 1)],
-        send_sem=tap_sem.at[0], recv_sem=tap_sem.at[1],
-        device_id=(lax.rem(me + 1, SHARDS), rep), device_id_type=MESH,
-    )
-    tap_all.wait_recv()
-    d_short[...] = jnp.sum(tap_recv[...], axis=0)
+    far_all.wait_recv()
+    d_short[...] = jnp.sum(far_recv[...], axis=0)
 
     for c in range(CHUNKS):
-        all_copies(send_in, recv_in, in_sem, c).wait_send()
-        all_copies(send_out, recv_out, out_sem, c).wait_send()
+        in_copies(c).wait_send()
+        out_copies(c, 0, SHARDS - 1).wait_send()
+
+        @pl.when(me < SHARDS - 1)
+        def _():
+            front_copy(c).wait_send()
 
         @pl.when(me > 0)
         def _():
             back_copy(c).wait_send()
 
     lag_all.wait_send()
-    tap_all.wait_send()
+    near_all.wait_send()
+    far_all.wait_send()
+
+
+def finish(d_rows, short, skips, lags, d_feat, d_short, d_skip, d_filt):
+    for pair in range(d_rows.shape[2] // 2):
+        rows = slice(16 * pair, 16 * pair + 16)
+        for j in range(3):
+            chunk = [
+                [d_rows[c, j, pair * 2 + u].astype(F32) for u in range(2)] for c in range(CHUNKS)
+            ]
+            for gp in range(2):
+                at = slice(8 * gp, 8 * gp + 8)
+                tiles = [swap_halves(chunk[0][u][at], chunk[1][u][at]) for u in range(2)]
+                for g in range(2):
+                    d_feat[j, 2 * gp + g, rows, :] = jnp.concatenate(
+                        [tiles[0][g], tiles[1][g]], axis=0
+                    ).astype(BF16)
+
+    @pl.when(pl.program_id(0) == 0)
+    def _():
+        turned = jnp.concatenate(
+            [short[...], jnp.zeros((LANES - 8, LANES), F32)], axis=0
+        ).T
+        wide = lax.broadcasted_iota(jnp.int32, (18, LANES), 1)
+        upper, lower = turned[0:18], turned[18:36]
+        members = (
+            jnp.where(wide < QUAD, upper, pltpu.roll(lower, QUAD, 1)),
+            jnp.where(wide < QUAD, pltpu.roll(upper, LANES - QUAD, 1), lower),
+        )
+        for j in range(3):
+            for i in range(3):
+                k = 3 * j + i
+                four = [members[g % 2][9 * (g // 2) + k : 9 * (g // 2) + k + 1] for g in range(4)]
+                d_short[j, i] = jnp.concatenate(four, axis=0)[:, 0:8]
+        flat = jnp.concatenate([skips[...], jnp.zeros((LANES - 32, LANES), F32)], axis=0).T[0:8]
+        four = []
+        for g in range(4):
+            first = flat if g == 0 else pltpu.roll(flat, LANES - 4 * g, 1)
+            second = pltpu.roll(flat, LANES - 12 - 4 * g, 1)
+            four.append(jnp.where(lane_ids() < QUAD, first, second)[0:1])
+        d_skip[...] = jnp.concatenate(four, axis=0)[:, 0:8]
+        for k in range(16):
+            d_filt[:, k * LANES : (k + 1) * LANES] = lags[pl.ds(k, 8, stride=16), :]
 
 
 def per_device(features, short_taps, skip_gain, filters, cotangent):
-    tap_rows = jnp.transpose(short_taps, (1, 0, 3, 2)).reshape(36, 512)
-    tap_rows = jnp.pad(tap_rows, ((0, 4), (0, 0)))
+    tap_rows = jnp.transpose(short_taps, (0, 3, 1, 2))
     vmem = pl.BlockSpec(memory_space=pltpu.VMEM)
     message = pltpu.VMEM((CHUNKS, SHARDS, 32, LANES), BF16)
-    d_feat, d_short, d_skip, d_filt = pl.pallas_call(
+    parts = pl.pallas_call(
         kernel,
         out_shape=(
-            jax.ShapeDtypeStruct((3, 4, 512, LANES), BF16),
+            jax.ShapeDtypeStruct((CHUNKS, 3, SHARDS, 16, LANES), BF16),
             jax.ShapeDtypeStruct((8, LANES), F32),
             jax.ShapeDtypeStruct((32, LANES), F32),
-            jax.ShapeDtypeStruct((8, 16, LANES), F32),
+            jax.ShapeDtypeStruct((128, LANES), F32),
         ),
         in_specs=[vmem, vmem, vmem, pl.BlockSpec(memory_space=pltpu.SMEM), vmem],
         out_specs=(vmem,) * 4,
@@ -659,15 +732,14 @@
             pltpu.VMEM((512, LANES), F32),
             pltpu.VMEM((8, LANES, LANES + 8192), BF16),
             pltpu.VMEM((8, LANES + 8192), F32),
-            pltpu.VMEM((6, 16, LANES), BF16),
-            pltpu.VMEM((6, 16, LANES), BF16),
-            pltpu.VMEM((6, 16, LANES), F32),
+            pltpu.VMEM((CHUNKS, 3, 16, LANES), BF16),
+            pltpu.VMEM((CHUNKS, 3, 16, LANES), BF16),
+            pltpu.VMEM((CHUNKS, 3, 16, LANES), F32),
             pltpu.VMEM((256, 256), BF16),
             pltpu.VMEM((LANES, 9 * LANES), BF16),
             pltpu.VMEM((256, 256), BF16),
-            pltpu.VMEM((256, 256), BF16),
-            pltpu.VMEM((256, LANES), BF16),
-            pltpu.VMEM((18 * LANES, LANES), BF16),
+            pltpu.VMEM((LANES, LANES), BF16),
+            pltpu.VMEM((9 * LANES, LANES), BF16),
             message, message, message, message,
             pltpu.VMEM((2, 1024, LANES), F32),
             pltpu.VMEM((2, 512, LANES), F32),
@@ -677,22 +749,29 @@
             pltpu.VMEM((2, 1024, LANES), F32),
             pltpu.VMEM((QUAD, 2, 4, 256, LANES), BF16),
             pltpu.VMEM((QUAD, LANES, 256), BF16),
+            pltpu.VMEM((QUAD, LANES, LANES), BF16),
             pltpu.VMEM((2, 4, LANES, 256), F32),
             pltpu.VMEM((QUAD, LAGS, 8, LANES), F32),
             pltpu.VMEM((QUAD, LAGS + 1, 8, LANES), F32),
             pltpu.VMEM((QUAD, 4, 16, LANES), F32),
             pltpu.VMEM((REPS, 8, 16, LANES), BF16),
             pltpu.VMEM((REPS, 8, 16, LANES), BF16),
-            pltpu.VMEM((CHUNKS, 3, SHARDS, 16, LANES), F32),
             pltpu.VMEM((CHUNKS, 3, SHARDS, 16, LANES), BF16),
+            pltpu.VMEM((CHUNKS, 3, 2, SHARDS, 16, LANES), BF16),
             pltpu.VMEM((CHUNKS, 3, 16, LANES), F32),
-            pltpu.VMEM((CHUNKS, 3, 16, LANES), F32),
+            pltpu.VMEM((CHUNKS, 3, 16, LANES), BF16),
+            pltpu.VMEM((CHUNKS, 3, 16, LANES), BF16),
             pltpu.VMEM((SHARDS, 8, LANES), F32),
-            pltpu.VMEM((SHARDS, 8, LANES), F32),
-            pltpu.SemaphoreType.DMA((2,)),
+            pltpu.VMEM((GROUP, 24, LANES), F32),
+            pltpu.VMEM((GROUP, 24, LANES), F32),
+            pltpu.VMEM((GROUP, 8, LANES), F32),
+            pltpu.VMEM((GROUP, 8, LANES), F32),
             pltpu.SemaphoreType.DMA((2, CHUNKS)),
             pltpu.SemaphoreType.DMA((2, CHUNKS)),
+            pltpu.SemaphoreType.DMA((CHUNKS,)),
+            pltpu.SemaphoreType.DMA((CHUNKS, GROUP)),
             pltpu.SemaphoreType.DMA((2, CHUNKS)),
+            pltpu.SemaphoreType.DMA((2,)),
             pltpu.SemaphoreType.DMA((2,)),
             pltpu.SemaphoreType.DMA((2,)),
         ],
@@ -700,10 +779,31 @@
             collective_id=0, has_side_effects=True, vmem_limit_bytes=60 * 2**20
         ),
     )(features, cotangent, tap_rows, skip_gain, filters)
-    short = d_short[:, :36].reshape(2, 4, 2, 2, 3, 3)
-    short = jnp.transpose(short, (4, 3, 0, 2, 1, 5)).reshape(3, 4, 8, 3)
-    skips = jnp.transpose(d_skip[:, 0].reshape(2, 4, 4), (1, 0, 2)).reshape(4, 8)
-    return (d_feat, short, skips, d_filt.reshape(8, 2048))
+    steps = 4
+    fixed = lambda *shape: pl.BlockSpec(shape, lambda i: (0,) * len(shape))
+    d_feat, short, skips, lags = pl.pallas_call(
+        finish,
+        grid=(steps,),
+        out_shape=(
+            jax.ShapeDtypeStruct((3, 4, 512, LANES), BF16),
+            jax.ShapeDtypeStruct((3, 3, 4, 8), F32),
+            jax.ShapeDtypeStruct((4, 8), F32),
+            jax.ShapeDtypeStruct((8, 2048), F32),
+        ),
+        in_specs=[
+            pl.BlockSpec((CHUNKS, 3, SHARDS // steps, 16, LANES), lambda i: (0, 0, i, 0, 0)),
+            fixed(8, LANES),
+            fixed(32, LANES),
+            fixed(128, LANES),
+        ],
+        out_specs=(
+            pl.BlockSpec((3, 4, 512 // steps, LANES), lambda i: (0, 0, i, 0)),
+            fixed(3, 3, 4, 8),
+            fixed(4, 8),
+            fixed(8, 2048),
+        ),
+    )(*parts)
+    return (d_feat, jnp.transpose(short, (0, 2, 3, 1)), skips, lags)
 
 
 def solution(mesh):

time: 110 us -> 92.6 us (0.84); the launches traced: 108 us -> 92.4 us
  local copies, waits for them, and re-layouts: 8.93 us -> 0 us
  Pallas kernels: 98.3 us -> 91.8 us
    pallas_call x1 -> x2, Pallas kernels: 98.3 us -> 91.8 us  [the longest x1 87.9 us: per_device(): pl.pallas_call(kernel, out_shape=(jax.ShapeDtypeStruct((CHUNKS, 3, SHARDS...]
    unnamed x2 -> x0, local copies, waits for them, and re-layouts: 4.14 us -> none
    slice x2 -> x0, local copies, waits for them, and re-layouts: 1.6 us -> none  [the longest x1 0.83 us: per_device(): d_skip[:, 0].reshape(2, 4, 4)]
    reshape x4 -> x0, local copies, waits for them, and re-layouts: 1.5 us -> none  [the longest x1 0.7 us: per_device(): short = jnp.transpose(short, (4, 3, 0, 2, 1, 5)).reshape(3, 4, 8, 3)]
where the time goes in v3:
time: 92.6 us; the launch traced here: 92.4 us
  Pallas kernels  91.8 us (99%)
    pallas_call x1, Pallas kernels, per_device(): pl.pallas_call(kernel, out_shape=(jax.ShapeDtypeStruct((CHUNKS, 3, SHARDS...  87.9 us
    pallas_call x1, Pallas kernels, per_device(): pl.pallas_call(finish, grid=(steps,), out_shape=(jax.ShapeDtypeStruct((3,...  3.91 us

profile of v3, /device:TPU:1, one launch (start us, length us, event | category | flops | bytes accessed | tf_op | source)
XLA Modules:
  0.0 92.4 jit_solution(14817771922411629335)
XLA Ops:
  0.6 87.9 %shard_map.84 = (bf16[2,3,64,16,128]{4,3,2,1,0:T(8,128)(2,1)}, f32[8,128]{1,0:T(8,128)}, f32[32,128]{1,0:T(8,128)}, f32[128,128]{1,0:T(8,128)}) custom-call(bf16[3,4,512,128]{3,2,1,0:T(8,128)(2,1)} %feat.1, bf16[4,512,128]{2,1,0:T(8,128)(2,1)} %cot.1, f32[3,3,4,512]{3,2,1,0:T(4,128)} %bitcast.2, f32[4,8]{1,0:T(4,128)} %skip.1, f32[8,8192]{1,0:T(8,128)} %filt.1), custom_call_target="tpu_custom_call" | custom-call | tf_op jit(solution)/shard_map/pallas_call | solution.py:718
  88.5 3.9 %shard_map.85 = (bf16[3,4,512,128]{3,2,1,0:T(8,128)(2,1)}, f32[3,3,4,8]{3,2,1,0:T(4,128)}, f32[4,8]{1,0:T(4,128)}, f32[8,2048]{1,0:T(8,128)}) custom-call(bf16[2,3,64,16,128]{4,3,2,1,0:T(8,128)(2,1)} %get-tuple-element.12.d_rows, f32[8,128]{1,0:T(8,128)} %get-tuple-element.13.short, f32[32,128]{1,0:T(8,128)} %get-tuple-element.14.skips, ...), custom_call_target="tpu_custom_call" | custom-call | tf_op jit(solution)/shard_map/pallas_call | solution.py:784

commit v4 on v3

--- a/solution.py
+++ b/solution.py
@@ -61,14 +61,14 @@
 
 def kernel(
     feat, cot, taps, skip, filt,
-    d_rows, d_short, d_skip, d_filt,
-    sig, mixed, wts, tcol, strip, base, front, front_in, halo,
+    d_out, d_short, d_skip, d_filt,
+    d_rows, sig, mixed, wts, tcol, strip, base, front, front_in, before_rows,
     m_early, m_col, m_late, m_first, m_sum,
     send_in, recv_in, send_out, recv_out,
     spread, prod_nat, grad_nat, xs, conv, merged,
     shifted, prod_t, prod_half, cross, low, high, lagrow, lag_send, lag_recv,
-    grads, early, back, back_out, back_in, taps_all, near_send, near_recv, far_send, far_recv,
-    front_sem, in_sem, out_sem, out_recv_sem, back_sem, near_sem, far_sem, lag_sem,
+    grads, early, back, back_out, back_in, taps_all, tap_send, tap_recv,
+    front_sem, in_sem, out_sem, out_recv_sem, back_sem, tap_sem, lag_sem, rows_sem,
 ):
     me = lax.axis_index("ctx")
     rep = lax.axis_index("rep")
@@ -88,14 +88,47 @@
             barrier, inc=1, device_id=(me, lax.rem(rep + k, REPS)), device_id_type=MESH
         )
 
+    zero = jnp.zeros((8, LANES), F32)
     row, col = ids(LANES, LANES)
     last = ones_where(row - (LANES - 2) == col % 2)
-    m_early[0:LANES, 0:LANES] = ones_where(col == row + 1)
-    m_early[0:LANES, LANES:] = ones_where(col == row + 2)
-    m_early[LANES:, 0:LANES] = ones_where((col == 0) & (row % 2 == 1))
-    m_early[LANES:, LANES:] = ones_where((col < 2) & (col == row % 2))
-    for k in range(9):
-        m_col[:, k * LANES : (k + 1) * LANES] = ones_where((row < 27) & (row % 9 == k))
+
+    owner = lax.shift_right_logical(ids(16, LANES)[1], 1)
+
+    def pack_front(j, _):
+        for gp in range(2):
+            tiles = []
+            for g in range(2):
+                spread_out = product_of(feat[j, 2 * gp + g], last)
+                tile = zero
+                for shard in range(SHARDS):
+                    tile = jnp.where(
+                        owner[0:8] == shard, spread_out[8 * shard : 8 * shard + 8], tile
+                    )
+                tiles.append(tile)
+            front[2 * j + gp] = jnp.concatenate(tiles, axis=0).astype(BF16)
+        return 0
+
+    lax.fori_loop(0, 3, pack_front, 0)
+
+    @pl.when(me == 0)
+    def _():
+        front_in[...] = jnp.zeros(front_in.shape, BF16)
+
+    @pl.when(me == SHARDS - 1)
+    def _():
+        back_in[...] = jnp.zeros(back_in.shape, BF16)
+
+    pl.semaphore_wait(barrier, SHARDS - 1 + REPS - 1)
+
+    def front_copy():
+        return pltpu.make_async_remote_copy(
+            src_ref=front, dst_ref=front_in, send_sem=front_sem.at[0], recv_sem=front_sem.at[1],
+            device_id=(lax.rem(me + 1, SHARDS), rep), device_id_type=MESH,
+        )
+
+    @pl.when(me < SHARDS - 1)
+    def _():
+        front_copy().start()
 
     def arrange(step, _):
         for half in range(4):
@@ -119,56 +152,26 @@
                         ).astype(BF16)
         return 0
 
-    zero = jnp.zeros((8, LANES), F32)
-    lax.fori_loop(0, SHARDS // 8, arrange, 0)
+
+    m_early[0:LANES, 0:LANES] = ones_where(col == row + 1)
+    m_early[0:LANES, LANES:] = ones_where(col == row + 2)
+    m_early[LANES:, 0:LANES] = ones_where((col == 0) & (row % 2 == 1))
+    m_early[LANES:, LANES:] = ones_where((col < 2) & (col == row % 2))
+    for k in range(9):
+        m_col[:, k * LANES : (k + 1) * LANES] = ones_where((row < 27) & (row % 9 == k))
 
     def eight(ref, *at):
         return ref[at].reshape(8 * 16, LANES)
 
-    def own_lanes(step):
-        rows, cols = ids(8 * 16, LANES)
-        return cols // 2 == step * 8 + rows // 16
-
-    def gather(values):
-        total = values[0:16]
-        for u in range(1, 8):
-            total = total + values[16 * u : 16 * u + 16]
-        return total
-
-    def pack_front(c, step, _):
-        mine = own_lanes(step)
-        shards = pl.ds(pl.multiple_of(step * 8, 8), 8)
-        for j in range(3):
-            spread_out = product_of(eight(sig, j, c, shards), last)
-            halo[c, j] += gather(jnp.where(mine, spread_out, 0.0))
-        return 0
-
-    halo[...] = jnp.zeros(halo.shape, F32)
-
-    def front_copy(c):
-        return pltpu.make_async_remote_copy(
-            src_ref=front.at[c], dst_ref=front_in.at[c], send_sem=front_sem.at[0, c],
-            recv_sem=front_sem.at[1, c], device_id=(lax.rem(me + 1, SHARDS), rep),
-            device_id_type=MESH,
-        )
-
-    @pl.when(me == 0)
-    def _():
-        front_in[...] = jnp.zeros(front_in.shape, BF16)
-
-    @pl.when(me == SHARDS - 1)
-    def _():
-        back_in[...] = jnp.zeros(back_in.shape, BF16)
-
-    for c in range(CHUNKS):
-        lax.fori_loop(0, SHARDS // 8, functools.partial(pack_front, c), 0)
-        front[c] = halo[c].astype(BF16)
-        if c == 0:
-            pl.semaphore_wait(barrier, SHARDS - 1 + REPS - 1)
-
-        @pl.when(me < SHARDS - 1)
-        def _():
-            front_copy(c).start()
+    def scatter(block, first):
+        return jnp.concatenate(
+            [jnp.where(owner == first + u, block, 0.0) for u in range(8)], axis=0
+        ).astype(BF16)
+
+    def gather(values, first, block):
+        for u in range(values.shape[0] // 16):
+            block = jnp.where(owner == first + u, values[16 * u : 16 * u + 16], block)
+        return block
 
     for part in range(4):
         cols = slice(part * LANES, (part + 1) * LANES)
@@ -200,7 +203,6 @@
                 wts[c, shard] = jnp.concatenate(made[c], axis=0).astype(BF16)
         return 0
 
-    lax.fori_loop(0, SHARDS // 8, arrange_taps, 0)
 
     def in_copy(c, peer):
         return pltpu.make_async_remote_copy(
@@ -240,13 +242,11 @@
     def short_conv(c, step, _):
         group = lax.rem(me // GROUP + step, SHARDS // GROUP)
         shards = pl.ds(pl.multiple_of(group * GROUP, GROUP), GROUP)
-        mine = own_lanes(group)
         weight = product_of(eight(wts, c, shards), m_col[...])
         mix = []
         for j in range(3):
             here = eight(sig, j, c, shards)
-            before = jnp.concatenate([front_in[c, j].astype(F32)] * 8, axis=0)
-            before = jnp.where(mine, before, 0.0).astype(BF16)
+            before = scatter(before_rows[c, j], group * GROUP)
             moved = product_of(jnp.concatenate([here, before], axis=1), m_early[...])
             for i in range(2):
                 early[c, j, i, shards] = (
@@ -272,13 +272,25 @@
 
         return 0
 
+    @pl.when(me > 0)
+    def _():
+        front_copy().wait_recv()
+
+    for j in range(3):
+        pairs = [front_in[2 * j + gp].astype(F32) for gp in range(2)]
+        pairs = [swap_halves(pair[0:8], pair[8:16]) for pair in pairs]
+        for c in range(CHUNKS):
+            before_rows[c, j] = jnp.concatenate([pairs[0][c], pairs[1][c]], axis=0)
+
+    def first_pass(step, _):
+        group = lax.rem(me // GROUP + step, SHARDS // GROUP)
+        arrange(group, 0)
+        arrange_taps(group, 0)
+        return short_conv(0, step, 0)
+
+    lax.fori_loop(0, SHARDS // GROUP, first_pass, 0)
+    lax.fori_loop(0, SHARDS // GROUP, functools.partial(short_conv, 1), 0)
     for c in range(CHUNKS):
-
-        @pl.when(me > 0)
-        def _():
-            front_copy(c).wait_recv()
-
-        lax.fori_loop(0, SHARDS // GROUP, functools.partial(short_conv, c), 0)
         recv_in[c, me] = send_in[c, me]
 
     strip[:, :, 0:LANES] = jnp.zeros((8, LANES, LANES), BF16)
@@ -503,18 +515,19 @@
 
     def make_grads(c, step, _):
         own = me // GROUP
-        group = lax.rem(own + GROUP - 1 - step, GROUP)
-
-        @pl.when(group == own)
-        def _():
-            out_copies(c, group, GROUP - 1).wait_recv()
-
-        @pl.when(group != own)
-        def _():
-            out_copies(c, group, GROUP).wait_recv()
-
-        shards = pl.ds(pl.multiple_of(group * 8, 8), 8)
-        mine = own_lanes(group)
+        pair = lax.rem(own // 2 + GROUP // 2 - 1 - step, GROUP // 2)
+        for half in range(2):
+            group = 2 * pair + half
+
+            @pl.when(group == own)
+            def _():
+                out_copies(c, group, GROUP - 1).wait_recv()
+
+            @pl.when(group != own)
+            def _():
+                out_copies(c, group, GROUP).wait_recv()
+
+        shards = pl.ds(pl.multiple_of(pair * 16, 16), 16)
         value = recv_out[c, shards, 16:32, :].astype(F32)
         three = (
             sig[3, c, shards].astype(F32) * recv_out[c, shards, 0:16, :].astype(F32),
@@ -525,20 +538,21 @@
         for j in range(3):
             narrow = three[j].astype(BF16)
             grads[c, j, shards] = narrow
-            spread_out = product_of(narrow.reshape(8 * 16, LANES), m_first[...])
-            back[c, j] += gather(jnp.where(mine, spread_out, 0.0))
-            wide = three[j].reshape(8 * 16, LANES)
-            terms.append((wide * eight(sig, j, c, shards).astype(F32)).astype(BF16))
+            spread_out = product_of(narrow.reshape(16 * 16, LANES), m_first[...])
+            back[c, j] = gather(spread_out, pair * 16, back[c, j])
+            terms.append((three[j] * sig[j, c, shards].astype(F32)).astype(BF16))
             for i in range(2):
-                terms.append((wide * eight(early, c, j, i, shards).astype(F32)).astype(BF16))
+                terms.append((three[j] * early[c, j, i, shards].astype(F32)).astype(BF16))
+        terms = [term.reshape(16 * 16, LANES) for term in terms]
         sums = product_of(jnp.concatenate(terms, axis=1), m_sum[...])
-        for u in range(8):
+        for u in range(16):
             first = sums[16 * u : 16 * u + 8]
             second = pltpu.roll(sums[16 * u + 8 : 16 * u + 16], 18 * c + 9, 1)
+            at = pl.ds(pl.multiple_of((pair * 16 + u) * 8, 8), 8)
             if c == 0:
-                taps_all[group * 8 + u] = first + second
+                taps_all[at, :] = first + second
             else:
-                taps_all[group * 8 + u] += pltpu.roll(first, 18 * c, 1) + second
+                taps_all[at, :] += pltpu.roll(first, 18 * c, 1) + second
         return 0
 
     def back_copy(c):
@@ -550,7 +564,7 @@
 
     def grads_of(c):
         back[c] = jnp.zeros(back.shape[1:], F32)
-        lax.fori_loop(0, SHARDS // GROUP, functools.partial(make_grads, c), 0)
+        lax.fori_loop(0, GROUP // 2, functools.partial(make_grads, c), 0)
         back_out[c] = back[c].astype(BF16)
 
         @pl.when(me > 0)
@@ -559,12 +573,10 @@
 
     def short_back(c, step, _):
         shards = pl.ds(pl.multiple_of(step * 8, 8), 8)
-        mine = own_lanes(step)
         weight = product_of(eight(wts, c, shards), m_col[...])
         for j in range(3):
             here = eight(grads, c, j, shards)
-            after = jnp.concatenate([back_in[c, j].astype(F32)] * 8, axis=0)
-            after = jnp.where(mine, after, 0.0).astype(BF16)
+            after = scatter(back_in[c, j].astype(F32), step * 8)
             moved = product_of(jnp.concatenate([here, after], axis=1), m_late[...])
             at = 3 * j * LANES
             total = (
@@ -582,58 +594,36 @@
 
         lax.fori_loop(0, SHARDS // GROUP, functools.partial(short_back, c), 0)
 
+    def rows_copy(c):
+        return pltpu.make_async_copy(d_rows.at[c], d_out.at[c], rows_sem.at[c])
+
     grads_of(0)
     features_of(0)
+    rows_copy(0).start()
     grads_of(1)
 
-    own_group = me // GROUP
-    own_place = lax.rem(me, GROUP)
-
-    def near_copy(place):
+    def tap_copy(peer):
         return pltpu.make_async_remote_copy(
-            src_ref=near_send.at[place], dst_ref=near_recv.at[own_place], send_sem=near_sem.at[0],
-            recv_sem=near_sem.at[1], device_id=(own_group * GROUP + place, rep),
-            device_id_type=MESH,
-        )
-
-    def far_copy(group):
-        return pltpu.make_async_remote_copy(
-            src_ref=far_send.at[group], dst_ref=far_recv.at[own_group], send_sem=far_sem.at[0],
-            recv_sem=far_sem.at[1], device_id=(group * GROUP + own_place, rep),
-            device_id_type=MESH,
-        )
-
-    for place in range(GROUP):
-        for m in range(3):
-            tile = taps_all[3 * m * GROUP + place]
-            for n in range(1, 3 if m < 2 else 2):
-                tile = tile + pltpu.roll(taps_all[(3 * m + n) * GROUP + place], 36 * n, 1)
-            near_send[place, 8 * m : 8 * m + 8, :] = tile
-    for k in range(1, GROUP):
-        near_copy(lax.rem(own_place + k, GROUP)).start()
-    near_recv[own_place] = near_send[own_place]
+            src_ref=tap_send.at[peer], dst_ref=tap_recv.at[me], send_sem=tap_sem.at[0],
+            recv_sem=tap_sem.at[1], device_id=(peer, rep), device_id_type=MESH,
+        )
+
+    for m in range(3):
+        total = taps_all[pl.ds(3 * m, SHARDS, stride=8), :]
+        for n in range(1, 3 if m < 2 else 2):
+            total = total + pltpu.roll(taps_all[pl.ds(3 * m + n, SHARDS, stride=8), :], 36 * n, 1)
+        tap_send[:, m, :] = total
+    tap_send[:, 3, :] = jnp.zeros((SHARDS, LANES), F32)
+
+    def send_taps(k, _):
+        tap_copy(lax.rem(me + k, SHARDS)).start()
+        return 0
+
+    lax.fori_loop(1, SHARDS, send_taps, 0)
+    tap_recv[me] = tap_send[me]
 
     features_of(1)
-
-    seven = pl.ds(0, GROUP - 1)
-    near_all = pltpu.make_async_remote_copy(
-        src_ref=near_send.at[seven], dst_ref=near_recv.at[seven], send_sem=near_sem.at[0],
-        recv_sem=near_sem.at[1], device_id=(lax.rem(me + 1, SHARDS), rep), device_id_type=MESH,
-    )
-    far_all = pltpu.make_async_remote_copy(
-        src_ref=far_send.at[seven], dst_ref=far_recv.at[seven], send_sem=far_sem.at[0],
-        recv_sem=far_sem.at[1], device_id=(lax.rem(me + 1, SHARDS), rep), device_id_type=MESH,
-    )
-    near_all.wait_recv()
-    packed = jnp.sum(near_recv[...], axis=0)
-    for group in range(GROUP):
-        tile = packed[8 * (group // 3) : 8 * (group // 3) + 8]
-        if group % 3:
-            tile = pltpu.roll(tile, LANES - 36 * (group % 3), 1)
-        far_send[group] = jnp.where(lane < 36, tile, 0.0)
-    for k in range(1, GROUP):
-        far_copy(lax.rem(own_group + k, GROUP)).start()
-    far_recv[own_group] = far_send[own_group]
+    rows_copy(1).start()
 
     lag_all = pltpu.make_async_remote_copy(
         src_ref=lag_send.at[pl.ds(0, REPS - 1)], dst_ref=lag_recv.at[pl.ds(0, REPS - 1)],
@@ -649,24 +639,30 @@
             + lag_recv[3, f].astype(F32)
         )
 
-    far_all.wait_recv()
-    d_short[...] = jnp.sum(far_recv[...], axis=0)
+    others = pl.ds(0, SHARDS - 1)
+    tap_all = pltpu.make_async_remote_copy(
+        src_ref=tap_send.at[others], dst_ref=tap_recv.at[others], send_sem=tap_sem.at[0],
+        recv_sem=tap_sem.at[1], device_id=(lax.rem(me + 1, SHARDS), rep), device_id_type=MESH,
+    )
+    tap_all.wait_recv()
+    d_short[0:4, :] = jnp.sum(tap_recv[...], axis=0)
+    d_short[4:8, :] = jnp.zeros((4, LANES), F32)
 
     for c in range(CHUNKS):
+        rows_copy(c).wait()
         in_copies(c).wait_send()
         out_copies(c, 0, SHARDS - 1).wait_send()
-
-        @pl.when(me < SHARDS - 1)
-        def _():
-            front_copy(c).wait_send()
 
         @pl.when(me > 0)
         def _():
             back_copy(c).wait_send()
 
     lag_all.wait_send()
-    near_all.wait_send()
-    far_all.wait_send()
+    tap_all.wait_send()
+
+    @pl.when(me < SHARDS - 1)
+    def _():
+        front_copy().wait_send()
 
 
 def finish(d_rows, short, skips, lags, d_feat, d_short, d_skip, d_filt):
@@ -686,8 +682,10 @@
 
     @pl.when(pl.program_id(0) == 0)
     def _():
+        moved = [short[...]] + [pltpu.roll(short[...], LANES - 36 * n, 1) for n in (1, 2)]
+        eight_rows = [moved[r % 3][r // 3 : r // 3 + 1] for r in range(8)]
         turned = jnp.concatenate(
-            [short[...], jnp.zeros((LANES - 8, LANES), F32)], axis=0
+            eight_rows + [jnp.zeros((LANES - 8, LANES), F32)], axis=0
         ).T
         wide = lax.broadcasted_iota(jnp.int32, (18, LANES), 1)
         upper, lower = turned[0:18], turned[18:36]
@@ -724,16 +722,17 @@
             jax.ShapeDtypeStruct((128, LANES), F32),
         ),
         in_specs=[vmem, vmem, vmem, pl.BlockSpec(memory_space=pltpu.SMEM), vmem],
-        out_specs=(vmem,) * 4,
+        out_specs=(pl.BlockSpec(memory_space=pl.ANY), vmem, vmem, vmem),
         scratch_shapes=[
+            pltpu.VMEM((CHUNKS, 3, SHARDS, 16, LANES), BF16),
             pltpu.VMEM((4, CHUNKS, SHARDS, 16, LANES), BF16),
             pltpu.VMEM((2, CHUNKS, SHARDS, 16, LANES), F32),
             pltpu.VMEM((CHUNKS, SHARDS, 16, LANES), BF16),
             pltpu.VMEM((512, LANES), F32),
             pltpu.VMEM((8, LANES, LANES + 8192), BF16),
             pltpu.VMEM((8, LANES + 8192), F32),
-            pltpu.VMEM((CHUNKS, 3, 16, LANES), BF16),
-            pltpu.VMEM((CHUNKS, 3, 16, LANES), BF16),
+            pltpu.VMEM((6, 16, LANES), BF16),
+            pltpu.VMEM((6, 16, LANES), BF16),
             pltpu.VMEM((CHUNKS, 3, 16, LANES), F32),
             pltpu.VMEM((256, 256), BF16),
             pltpu.VMEM((LANES, 9 * LANES), BF16),
@@ -761,25 +760,23 @@
             pltpu.VMEM((CHUNKS, 3, 16, LANES), F32),
             pltpu.VMEM((CHUNKS, 3, 16, LANES), BF16),
             pltpu.VMEM((CHUNKS, 3, 16, LANES), BF16),
-            pltpu.VMEM((SHARDS, 8, LANES), F32),
-            pltpu.VMEM((GROUP, 24, LANES), F32),
-            pltpu.VMEM((GROUP, 24, LANES), F32),
-            pltpu.VMEM((GROUP, 8, LANES), F32),
-            pltpu.VMEM((GROUP, 8, LANES), F32),
-            pltpu.SemaphoreType.DMA((2, CHUNKS)),
+            pltpu.VMEM((SHARDS * 8, LANES), F32),
+            pltpu.VMEM((SHARDS, 4, LANES), F32),
+            pltpu.VMEM((SHARDS, 4, LANES), F32),
+            pltpu.SemaphoreType.DMA((2,)),
             pltpu.SemaphoreType.DMA((2, CHUNKS)),
             pltpu.SemaphoreType.DMA((CHUNKS,)),
             pltpu.SemaphoreType.DMA((CHUNKS, GROUP)),
             pltpu.SemaphoreType.DMA((2, CHUNKS)),
             pltpu.SemaphoreType.DMA((2,)),
             pltpu.SemaphoreType.DMA((2,)),
-            pltpu.SemaphoreType.DMA((2,)),
+            pltpu.SemaphoreType.DMA((CHUNKS,)),
         ],
         compiler_params=pltpu.CompilerParams(
             collective_id=0, has_side_effects=True, vmem_limit_bytes=60 * 2**20
         ),
     )(features, cotangent, tap_rows, skip_gain, filters)
-    steps = 4
+    steps = 2
     fixed = lambda *shape: pl.BlockSpec(shape, lambda i: (0,) * len(shape))
     d_feat, short, skips, lags = pl.pallas_call(
         finish,

time: 92.6 us -> 89.6 us (0.968)
  Pallas kernels: 91.8 us -> 88.8 us
    pallas_call x1, Pallas kernels: 87.9 us -> 86.1 us  [per_device(): pl.pallas_call(kernel, out_shape=(jax.ShapeDtypeStruct((CHUNKS, 3, SHARDS...]
    pallas_call x1, Pallas kernels: 3.91 us -> 2.73 us  [per_device(): pl.pallas_call(finish, grid=(steps,), out_shape=(jax.ShapeDtypeStruct((3,...]
where the time goes in v4:
time: 89.6 us; the launch traced here: 89.5 us
  Pallas kernels  88.8 us (99%)
    pallas_call x1, Pallas kernels, per_device(): pl.pallas_call(kernel, out_shape=(jax.ShapeDtypeStruct((CHUNKS, 3, SHARDS...  86.1 us
    pallas_call x1, Pallas kernels, per_device(): pl.pallas_call(finish, grid=(steps,), out_shape=(jax.ShapeDtypeStruct((3,...  2.73 us

profile of v4, /device:TPU:1, one launch (start us, length us, event | category | flops | bytes accessed | tf_op | source)
XLA Modules:
  0.0 89.5 jit_solution(17897438620066982677)
XLA Ops:
  0.6 86.1 %shard_map.84 = (bf16[2,3,64,16,128]{4,3,2,1,0:T(8,128)(2,1)}, f32[8,128]{1,0:T(8,128)}, f32[32,128]{1,0:T(8,128)}, f32[128,128]{1,0:T(8,128)}) custom-call(bf16[3,4,512,128]{3,2,1,0:T(8,128)(2,1)} %feat.1, bf16[4,512,128]{2,1,0:T(8,128)(2,1)} %cot.1, f32[3,3,4,512]{3,2,1,0:T(4,128)} %bitcast.2, f32[4,8]{1,0:T(4,128)} %skip.1, f32[8,8192]{1,0:T(8,128)} %filt.1), custom_call_target="tpu_custom_call" | custom-call | tf_op jit(solution)/shard_map/pallas_call | solution.py:716
  86.8 2.7 %shard_map.85 = (bf16[3,4,512,128]{3,2,1,0:T(8,128)(2,1)}, f32[3,3,4,8]{3,2,1,0:T(4,128)}, f32[4,8]{1,0:T(4,128)}, f32[8,2048]{1,0:T(8,128)}) custom-call(bf16[2,3,64,16,128]{4,3,2,1,0:T(8,128)(2,1)} %get-tuple-element.12.d_rows, f32[8,128]{1,0:T(8,128)} %get-tuple-element.13.short, f32[32,128]{1,0:T(8,128)} %get-tuple-element.14.skips, ...), custom_call_target="tpu_custom_call" | custom-call | tf_op jit(solution)/shard_map/pallas_call | solution.py:781

commit v5 on v4

--- a/solution.py
+++ b/solution.py
@@ -598,8 +598,6 @@
         return pltpu.make_async_copy(d_rows.at[c], d_out.at[c], rows_sem.at[c])
 
     grads_of(0)
-    features_of(0)
-    rows_copy(0).start()
     grads_of(1)
 
     def tap_copy(peer):
@@ -622,8 +620,9 @@
     lax.fori_loop(1, SHARDS, send_taps, 0)
     tap_recv[me] = tap_send[me]
 
-    features_of(1)
-    rows_copy(1).start()
+    for c in range(CHUNKS):
+        features_of(c)
+        rows_copy(c).start()
 
     lag_all = pltpu.make_async_remote_copy(
         src_ref=lag_send.at[pl.ds(0, REPS - 1)], dst_ref=lag_recv.at[pl.ds(0, REPS - 1)],

time: 89.6 us -> 84.5 us (0.943)
  the two profiles are of different devices: /device:TPU:1 before, /device:TPU:33 now
where the time goes in v5:
time: 84.5 us; the launch traced here: 84.3 us
  Pallas kernels  83.7 us (99%)
    pallas_call x1, Pallas kernels, per_device(): pl.pallas_call(kernel, out_shape=(jax.ShapeDtypeStruct((CHUNKS, 3, SHARDS...  81 us
    pallas_call x1, Pallas kernels, per_device(): pl.pallas_call(finish, grid=(steps,), out_shape=(jax.ShapeDtypeStruct((3,...  2.73 us

profile of v5, /device:TPU:33, one launch (start us, length us, event | category | flops | bytes accessed | tf_op | source)
XLA Modules:
  0.0 84.3 jit_solution(7830686091774429565)
XLA Ops:
  0.6 81.0 %shard_map.84 = (bf16[2,3,64,16,128]{4,3,2,1,0:T(8,128)(2,1)}, f32[8,128]{1,0:T(8,128)}, f32[32,128]{1,0:T(8,128)}, f32[128,128]{1,0:T(8,128)}) custom-call(bf16[3,4,512,128]{3,2,1,0:T(8,128)(2,1)} %feat.1, bf16[4,512,128]{2,1,0:T(8,128)(2,1)} %cot.1, f32[3,3,4,512]{3,2,1,0:T(4,128)} %bitcast.2, f32[4,8]{1,0:T(4,128)} %skip.1, f32[8,8192]{1,0:T(8,128)} %filt.1), custom_call_target="tpu_custom_call" | custom-call | tf_op jit(solution)/shard_map/pallas_call | solution.py:715
  81.6 2.7 %shard_map.85 = (bf16[3,4,512,128]{3,2,1,0:T(8,128)(2,1)}, f32[3,3,4,8]{3,2,1,0:T(4,128)}, f32[4,8]{1,0:T(4,128)}, f32[8,2048]{1,0:T(8,128)}) custom-call(bf16[2,3,64,16,128]{4,3,2,1,0:T(8,128)(2,1)} %get-tuple-element.12.d_rows, f32[8,128]{1,0:T(8,128)} %get-tuple-element.13.short, f32[32,128]{1,0:T(8,128)} %get-tuple-element.14.skips, ...), custom_call_target="tpu_custom_call" | custom-call | tf_op jit(solution)/shard_map/pallas_call | solution.py:780

commit v6 on v5

--- a/solution.py
+++ b/solution.py
@@ -446,7 +446,7 @@
             low[q, 8 * m + lag] = kept
             high[q, 8 * m + lag] = total - kept
 
-    def owner_lags(c):
+    def lag_blocks(c):
         for q in range(QUAD):
             for e in range(2):
                 prod_t[q, :, LANES * e : LANES * e + LANES] = (
@@ -459,6 +459,8 @@
                     shifted[q, e, k, 0:128, :] = grad_nat[
                         e, pl.ds(q + 16 * k, 128, stride=4), :
                     ].astype(BF16)
+
+    def owner_lags(c):
         cross_dots(0, 0, 0)
 
         def one_filter(q, _):
@@ -499,8 +501,10 @@
                 lag_send[r, QUAD * c + q] = turned[16 * r : 16 * r + 16]
 
     owner_conv(0)
+    lag_blocks(0)
+    owner_conv(1)
     owner_lags(0)
-    owner_conv(1)
+    lag_blocks(1)
     owner_lags(1)
 
     def lag_copy(peer):

time: 84.5 us -> 80.8 us (0.956)
  the two profiles are of different devices: /device:TPU:33 before, /device:TPU:1 now
where the time goes in v6:
time: 80.8 us; the launch traced here: 79.2 us
  Pallas kernels  78.6 us (97%)
    pallas_call x1, Pallas kernels, per_device(): pl.pallas_call(kernel, out_shape=(jax.ShapeDtypeStruct((CHUNKS, 3, SHARDS...  75.9 us
    pallas_call x1, Pallas kernels, per_device(): pl.pallas_call(finish, grid=(steps,), out_shape=(jax.ShapeDtypeStruct((3,...  2.73 us

profile of v6, /device:TPU:1, one launch (start us, length us, event | category | flops | bytes accessed | tf_op | source)
XLA Modules:
  0.0 79.2 jit_solution(750658912766295287)
XLA Ops:
  0.6 75.9 %shard_map.84 = (bf16[2,3,64,16,128]{4,3,2,1,0:T(8,128)(2,1)}, f32[8,128]{1,0:T(8,128)}, f32[32,128]{1,0:T(8,128)}, f32[128,128]{1,0:T(8,128)}) custom-call(bf16[3,4,512,128]{3,2,1,0:T(8,128)(2,1)} %feat.1, bf16[4,512,128]{2,1,0:T(8,128)(2,1)} %cot.1, f32[3,3,4,512]{3,2,1,0:T(4,128)} %bitcast.2, f32[4,8]{1,0:T(4,128)} %skip.1, f32[8,8192]{1,0:T(8,128)} %filt.1), custom_call_target="tpu_custom_call" | custom-call | tf_op jit(solution)/shard_map/pallas_call | solution.py:719
  76.5 2.7 %shard_map.85 = (bf16[3,4,512,128]{3,2,1,0:T(8,128)(2,1)}, f32[3,3,4,8]{3,2,1,0:T(4,128)}, f32[4,8]{1,0:T(4,128)}, f32[8,2048]{1,0:T(8,128)}) custom-call(bf16[2,3,64,16,128]{4,3,2,1,0:T(8,128)(2,1)} %get-tuple-element.12.d_rows, f32[8,128]{1,0:T(8,128)} %get-tuple-element.13.short, f32[32,128]{1,0:T(8,128)} %get-tuple-element.14.skips, ...), custom_call_target="tpu_custom_call" | custom-call | tf_op jit(solution)/shard_map/pallas_call | solution.py:784
